TPU v7x, 32 devices: a whole 2x2x4 slice. The times are simulated.
32 devices in a mesh: rec: 8 (over y, x, core), rot: 4 (over z).
Axes of the slice: x: 2, y: 2, z: 4, core: 2. Of those that a mesh axis runs over, the one named last changes fastest.
Arguments:
- receptors: bfloat16 [64, 60, 900], P('rec'), may hold values from -0.09375 to 0.09375
- ligands: bfloat16 [64, 60, 900], P('rec'), may hold values from -6 to 6
- wigner: bfloat16 [32, 35990], P('rot')
- trans_table: bfloat16 [16, 30, 30, 30], replicated, may hold values from -1 to 1
- dist_index: int32 [8], replicated, may hold values from 0 to 15, as said below
Outputs:
- energy: float32 [64, 64], P('rec', 'rot')
Inputs may be any that keep to these rules, and one draw needn't show every extreme that they name: `dist_index`: indices into the tabulated distances; the first and the last tabulated distance are both among them.
All inputs are finite; a program needn't handle non-finite values.
Results may differ from a plain program's by a relative error of at most 0.0035.
Values may be sent and summed in bfloat16 or wider, within the bound.
A program may use at most 192 MiB of HBM per device.

v0:
```python
import math

import jax
import jax.numpy as jnp
from jax import lax
from jax.sharding import PartitionSpec as P


def packed_start(degree):
    return degree * (4 * degree * degree - 1) // 3


def translate_parts(coeffs, tables):
    numrows = coeffs.shape[0]
    radial = tables.shape[2]
    split_rows = coeffs.reshape(numrows, coeffs.shape[1] // radial, radial, coeffs.shape[2])
    parts = []
    for degree in range(tables.shape[1]):
        column_lo = degree * degree
        extent = 2 * degree + 1
        window = split_rows[..., column_lo : column_lo + extent]
        piece = jnp.einsum(
            "tji,rpic->trpjc", tables[:, degree], window, preferred_element_type=jnp.float32
        )
        parts.append(piece.astype(jnp.bfloat16).reshape(tables.shape[0] * numrows, -1))
    return parts


def rotate_parts(coeffs, wigner):
    degrees = math.isqrt(coeffs.shape[2])
    parts = []
    for degree in range(degrees):
        extent = 2 * degree + 1
        offset = packed_start(degree)
        window = coeffs[..., degree * degree : degree * degree + extent]
        matrix = wigner[:, offset : offset + extent * extent].reshape(
            wigner.shape[0], extent, extent
        )
        piece = jnp.einsum("gxm,qmk->qgxk", window, matrix, preferred_element_type=jnp.float32)
        parts.append(piece.astype(jnp.bfloat16).reshape(wigner.shape[0] * coeffs.shape[0], -1))
    return parts


def weight_sums(trans_parts, rot_parts, dist_count, rec_count, rot_count, lig_count):
    score = jnp.zeros((dist_count * rec_count, rot_count * lig_count), jnp.float32)
    for left_part, right_part in zip(trans_parts, rot_parts):
        score = score + lax.dot_general(
            left_part, right_part, (((1,), (1,)), ((), ())), preferred_element_type=jnp.float32
        )
    weights = jnp.exp(score).reshape(dist_count, rec_count, rot_count, lig_count)
    return jnp.sum(weights, axis=(0, 2))


def per_device(receptors, ligands, wigner, trans_table, dist_index):
    tables = trans_table[dist_index]
    dist_count = tables.shape[0]
    rec_count = receptors.shape[0]
    trans_parts = translate_parts(receptors, tables)
    shard_piece = lax.all_gather(ligands, "rec", axis=0, tiled=True)
    row_count = shard_piece.shape[0]
    grouping = math.gcd(row_count, 8)
    stacked = shard_piece.reshape(
        row_count // grouping, grouping, shard_piece.shape[1], shard_piece.shape[2]
    )

    def one_group(lgroup):
        return weight_sums(
            trans_parts,
            rotate_parts(lgroup, wigner),
            dist_count,
            rec_count,
            wigner.shape[0],
            grouping,
        )

    partial_sums = lax.map(one_group, stacked)
    local_sums = jnp.moveaxis(partial_sums, 0, 1).reshape(rec_count, row_count)
    totals = lax.psum(local_sums, "rot")
    share_cols = totals.shape[1] // lax.axis_size("rot")
    totals = lax.dynamic_slice_in_dim(totals, lax.axis_index("rot") * share_cols, share_cols, 1)
    return jnp.log(totals)


def solution(mesh):
    in_specs = (P("rec", None, None), P("rec", None, None), P("rot", None), P(), P())
    out_specs = P("rec", "rot")
    return jax.shard_map(
        per_device, mesh=mesh, in_specs=in_specs, out_specs=out_specs, check_vma=False
    )
```

profile of v0, /device:TPU:0, one launch (start us, length us, event | category | flops | bytes accessed | tf_op | source)
XLA Modules:
  0.0 1378.7 jit_solution(12588348215441555630)
XLA Ops:
  29.7 5.4 gather_fusion
  42.6 2.2 reshape.466
  47.2 2.8 reshape.307
  53.2 2.2 reshape.308
  58.7 2.2 reshape.309
  64.3 2.3 reshape.310
  67.7 2.1 fusion.100
  69.8 2.2 copy.402
  72.0 2.2 reshape.311
  75.7 2.2 copy.405
  77.9 2.2 reshape.312
  81.6 2.1 copy.408
  83.8 2.2 reshape.313
  88.1 2.2 reshape.314
  90.7 2.2 reshape.315
  93.4 2.3 reshape.316
  96.1 2.3 reshape.317
  98.8 2.3 reshape.318
  101.5 2.3 reshape.319
  104.2 2.5 reshape.320
  107.2 2.2 reshape.321
  109.8 2.3 reshape.322
  112.5 2.2 reshape.323
  115.1 2.3 reshape.324
  117.8 2.3 reshape.325
  120.5 2.6 reshape.326
  123.5 2.6 reshape.327
  126.6 2.2 reshape.328
  129.2 2.2 reshape.329
  131.8 2.2 reshape.330
  134.4 2.3 reshape.331
  137.1 2.3 reshape.332
  139.4 17.2 %copy.375 = bf16[64,60,900]{1,2,0:T(8,128)(2,1)} copy(bf16[64,60,900]{2,0,1:T(8,128)(2,1)} %all-gather.2.cloned.1.call-done) | data formatting | bytes 13824000 | tf_op jit(solution)/shard_map/all_gather | solution.py:59
  156.7 1200.0 %while.10 = (s32[]{:T(128)}, f32[8,8,8]{2,1,0:T(8,128)}, bf16[8,8,60,900]{2,3,1,0:T(8,128)(2,1)}, bf16[8,35990]{1,0:T(8,128)(2,1)}, bf16[64,60]{1,0:T(8,128)(2,1...) while((s32[]{:T(128)}, f32[8,8,8]{2,1,0:T(8,128)}, ...), condition=%wide.region_2.3_spmd, body=%wide.region_0.2_spmd.sunk | while | flops 722346688 | bytes 64573340 | solution.py:76
  197.5 1.9 reshape.542
  240.0 1.8 fusion.446
  251.4 1.9 copy.779
  285.9 2.2 copy.784
  347.4 1.9 reshape.542
  389.9 1.8 fusion.446
  401.2 1.9 copy.779
  435.7 2.2 copy.784
  497.2 1.9 reshape.542
  539.8 1.8 fusion.446
  551.1 1.9 copy.779
  585.6 2.2 copy.784
  647.1 1.9 reshape.542
  689.6 1.8 fusion.446
  700.9 1.9 copy.779
  735.4 2.2 copy.784
  797.0 1.9 reshape.542
  839.5 1.8 fusion.446
  850.8 1.9 copy.779
  885.3 2.2 copy.784
  946.8 1.9 reshape.542
  1000.7 1.9 copy.779
  1035.2 2.2 copy.784
  1096.7 1.9 reshape.542
  1150.5 1.9 copy.779
  1185.0 2.2 copy.784
  1246.5 1.9 reshape.542
  1300.4 1.9 copy.779
  1334.9 2.2 copy.784
  1357.5 13.5 psum.7
  (1835 shorter events, 1191.2 us)
Async XLA Ops:
  6.5 132.9 %all-gather.2.cloned.1.call-start = ((), (), s32[]{:S(2)}) async-start(), calls=%async_computation | async-start | bytes 8847360 | tf_op jit(solution)/shard_map/all_gather | solution.py:59
  18.9 10.9 copy-start.38
  67.7 6.5 copy-start.35
  74.4 5.7 copy-start.34
  80.4 5.7 copy-start.33
  98.8 5.1 copy-start.27
  101.5 5.3 copy-start.26
  104.2 5.2 copy-start.25
  117.8 5.3 copy-start.20
  120.5 5.7 copy-start.19
  123.5 5.3 copy-start.18
  193.9 5.6 copy-start.3
  195.7 5.4 copy-start.15
  196.9 6.1 copy-start.14
  197.5 7.7 copy-start.13
  213.1 5.0 copy-start.7
  229.6 5.1 copy-start.4
  229.6 5.1 copy-start.9
  343.7 5.6 copy-start.3
  345.5 5.4 copy-start.15
  346.8 6.1 copy-start.14
  347.4 7.7 copy-start.13
  363.0 5.0 copy-start.7
  379.4 5.1 copy-start.4
  379.4 5.1 copy-start.9
  493.6 5.6 copy-start.3
  495.4 5.4 copy-start.15
  496.6 6.1 copy-start.14
  497.2 7.7 copy-start.13
  529.3 5.1 copy-start.4
  529.3 5.1 copy-start.9
  643.5 5.6 copy-start.3
  645.3 5.4 copy-start.15
  646.5 6.1 copy-start.14
  647.1 7.7 copy-start.13
  662.7 5.0 copy-start.7
  679.1 5.1 copy-start.4
  679.1 5.1 copy-start.9
  793.3 5.6 copy-start.3
  795.1 5.4 copy-start.15
  796.3 6.1 copy-start.14
  796.9 7.7 copy-start.13
  829.0 5.1 copy-start.4
  829.0 5.1 copy-start.9
  943.2 5.6 copy-start.3
  945.0 5.4 copy-start.15
  946.2 6.1 copy-start.14
  946.8 7.7 copy-start.13
  962.4 5.0 copy-start.7
  978.8 5.1 copy-start.4
  978.9 5.1 copy-start.9
  1093.0 5.6 copy-start.3
  1094.8 5.4 copy-start.15
  1096.0 6.1 copy-start.14
  1096.7 7.7 copy-start.13
  1112.3 5.0 copy-start.7
  1128.7 5.1 copy-start.4
  1128.7 5.1 copy-start.9
  1242.9 5.6 copy-start.3
  1244.7 5.4 copy-start.15
  1245.9 6.1 copy-start.14
  1246.5 7.7 copy-start.13
  1278.6 5.1 copy-start.4
  1278.6 5.1 copy-start.9
  (81 other events, 307.0 us)
Sparse Core Ops, SparseCore 0:
  9.3 54.9 all-gather.1
where the time goes:
time: 1410 us; the launch traced here: 1380 us
  local copies, waits for them, and re-layouts  922 us (65%)
  matrix products  412 us (29%)
  between operations  14.1 us (1%)
    reshape x232, local copies, waits for them, and re-layouts, rotate_parts(): piece.astype(jnp.bfloat16).reshape(wigner.shape[0] * coeffs.shape[0], -1)  332 us
    dot_general x240, matrix products, weight_sums(): lax.dot_general(left_part, right_part, (((1,), (1,)), ((), ())), preferre...  256 us
    convert_element_type x232, local copies, waits for them, and re-layouts, rotate_parts(): piece.astype(jnp.bfloat16).reshape(wigner.shape[0] * coeffs.shape[0], -1)  215 us
    slice x232, local copies, waits for them, and re-layouts, rotate_parts(): wigner[:, offset:offset + extent * extent]  188 us
    dot_general x232, matrix products, rotate_parts(): jnp.einsum('gxm,qmk->qgxk', window, matrix, preferred_element_type=jnp.fl...  138 us
    reshape x29, local copies, waits for them, and re-layouts, translate_parts(): piece.astype(jnp.bfloat16).reshape(tables.shape[0] * numrows, -1)  61.3 us
    reshape x256, local copies, waits for them, and re-layouts, rotate_parts(): wigner[:, offset:offset + extent * extent]  35.3 us
  transfers between devices with their start and end apart: 1, of which 0 were waited for; matrix products, arithmetic and copies ran while one was open for 10% of the time, Pallas kernels for 0%

commit v1 on v0

v1 whole, which is shorter than its diff:
```python
import functools
import math

import jax
import jax.numpy as jnp
from jax import lax
from jax.experimental import pallas as pl
from jax.experimental.pallas import tpu as pltpu
from jax.sharding import PartitionSpec as P

SLOT = 64


def packed_start(degree):
    return degree * (4 * degree * degree - 1) // 3


def degree_groups(degrees):
    left = list(range(degrees))
    groups = []
    while left:
        members = [left.pop()]
        used = 2 * members[0] + 1
        while left:
            fits = [d for d in left if used + 2 * d + 1 <= SLOT]
            if not fits:
                break
            pick = fits[-1]
            left.remove(pick)
            members.append(pick)
            used += 2 * pick + 1
        groups.append(members)
    return groups


def slot_columns(array, groups):
    parts = []
    for members in groups:
        used = 0
        for d in members:
            parts.append(array[..., d * d : d * d + 2 * d + 1])
            used += 2 * d + 1
        if used < SLOT:
            parts.append(jnp.zeros(array.shape[:-1] + (SLOT - used,), array.dtype))
    joined = jnp.concatenate(parts, axis=-1)
    return joined.reshape(array.shape[:-1] + (len(groups), SLOT))


def unpack_kernel(groups, front, w_ref, out_ref, scr):
    rows = w_ref.shape[0]
    lane = lax.broadcasted_iota(jnp.int32, (rows, 128), 1)
    for index, members in enumerate(groups):
        used = 0
        for d in members:
            extent = 2 * d + 1
            keep = (lane >= used) & (lane < used + extent)
            for m in range(extent):
                start = front + packed_start(d) + m * extent - used
                base = start // 128 * 128
                window = w_ref[:, base : base + 256].astype(jnp.float32)
                shift = start - base
                if shift:
                    window = pltpu.roll(window, 256 - shift, 1)
                scr[:, used + m, :] = jnp.where(keep, window[:, :128], 0.0)
            used += extent
        for m in range(used, SLOT):
            scr[:, m, :] = jnp.zeros((rows, 128), jnp.float32)
        out_ref[index] = scr[...].astype(jnp.bfloat16)


def unpack_wigner(wigner, groups):
    front = 128
    rows, width = wigner.shape
    total = (front + width + 127) // 128 * 128 + 256
    padded = jnp.pad(wigner, ((0, 0), (front, total - front - width)))
    qstep = 8 if rows % 16 else 16
    return pl.pallas_call(
        functools.partial(unpack_kernel, groups, front),
        grid=(rows // qstep,),
        in_specs=[pl.BlockSpec((qstep, total), lambda i: (i, 0))],
        out_specs=pl.BlockSpec((len(groups), qstep, SLOT, 128), lambda i: (0, i, 0, 0)),
        out_shape=jax.ShapeDtypeStruct((len(groups), rows, SLOT, 128), jnp.bfloat16),
        scratch_shapes=[pltpu.VMEM((qstep, SLOT, 128), jnp.float32)],
        compiler_params=pltpu.CompilerParams(vmem_limit_bytes=48 * 1024 * 1024),
        name="unpack",
    )(padded)


def score_kernel(tab_ref, rec_ref, lig_ref, wig_ref, out_ref, trans, rot, acc):
    step = pl.program_id(0)
    rad = lig_ref.shape[1]
    ligs = lig_ref.shape[2]
    rots = wig_ref.shape[1]
    dists = tab_ref.shape[1] // (2 * rad)
    recs = rec_ref.shape[2] // 128

    @pl.when(step == 0)
    def _():
        acc[...] = jnp.zeros_like(acc)

    moved = jnp.dot(tab_ref[0], rec_ref[0], preferred_element_type=jnp.float32)
    moved = moved.reshape(2, rad, dists, recs * 128)
    for xq in range(rad):
        for half in range(2):
            piece = jnp.concatenate(
                [moved[half, xq, :, r * 128 : (r + 1) * 128] for r in range(recs)], axis=0
            )
            lo = xq * 256 + half * 128
            trans[:, lo : lo + 128] = piece.astype(jnp.bfloat16)

    coeffs = lig_ref[0].reshape(rad * ligs, 256)
    lane = lax.broadcasted_iota(jnp.int32, (SLOT, 128), 1)
    zero = jnp.zeros((SLOT, 128), jnp.bfloat16)

    def one_rotation(q, carry):
        block = wig_ref[0, q]
        wide = block.astype(jnp.float32)
        other = pltpu.roll(wide, SLOT, 1).astype(jnp.bfloat16)
        pair = jnp.concatenate([block, other], axis=0)
        none = jnp.concatenate([zero, zero], axis=0)
        full = jnp.concatenate(
            [jnp.concatenate([pair, none], axis=1), jnp.concatenate([none, pair], axis=1)], axis=0
        )
        turned = jnp.dot(coeffs, full, preferred_element_type=jnp.float32).astype(jnp.bfloat16)
        row = pl.multiple_of(q * ligs, 16)
        for xq in range(rad):
            rot[pl.ds(row, ligs), xq * 256 : (xq + 1) * 256] = turned[xq * ligs : (xq + 1) * ligs]
        return carry

    lax.fori_loop(0, rots, one_rotation, 0, unroll=4)

    acc[...] += lax.dot_general(
        rot[...], trans[...], (((1,), (1,)), ((), ())), preferred_element_type=jnp.float32
    )

    @pl.when(step == pl.num_programs(0) - 1)
    def _():
        weights = jnp.exp(acc[...])
        out_ref[...] = jnp.sum(weights.reshape(rots, ligs, acc.shape[1]), axis=0)


def per_device(receptors, ligands, wigner, trans_table, dist_index):
    degrees = trans_table.shape[1]
    radial = trans_table.shape[2]
    half = radial // 2
    groups = degree_groups(degrees)
    count = len(groups)
    recs, rows, _ = receptors.shape
    props = rows // radial
    dists = dist_index.shape[0]
    nrec = lax.axis_size("rec")
    nrot = lax.axis_size("rot")
    per_col = nrec // nrot
    local_ligs = ligands.shape[0]
    ligs = local_ligs * per_col

    lig = slot_columns(ligands, groups).reshape(local_ligs, props, 2, half, count, SLOT)
    lig = jnp.transpose(lig, (4, 3, 0, 2, 1, 5)).reshape(count * half * local_ligs, 256)
    share = -(-lig.shape[0] // (16 * nrec)) * 16
    used = lig.shape[0]
    pieces = jnp.pad(lig, ((0, share * nrec - used), (0, 0))).reshape(nrec, share, 256)
    spread = lax.all_to_all(pieces, "rec", 0, 0, tiled=False)
    mine = lax.dynamic_slice_in_dim(spread, lax.axis_index("rot") * per_col, per_col, 0)
    whole = lax.all_gather(mine, "rec", axis=1, tiled=False)
    whole = whole.reshape(per_col, nrec * share, 256)[:, :used]
    whole = whole.reshape(per_col, count, half, local_ligs, 256)
    whole = jnp.moveaxis(whole, 0, 2).reshape(count, half, ligs, 256)

    turns = lax.all_gather(wigner, "rot", axis=0, tiled=True)
    rots = turns.shape[0]
    wig = unpack_wigner(turns, groups)

    most = max(len(members) for members in groups)
    depth = most * radial
    rec = slot_columns(receptors, groups).reshape(recs, props, radial, count, SLOT)
    rec = jnp.transpose(rec, (3, 2, 0, 1, 4))
    tables = jnp.transpose(trans_table[dist_index], (1, 2, 0, 3))
    owner = []
    index = []
    for members in groups:
        row = []
        for place, d in enumerate(members):
            row += [place] * (2 * d + 1)
        owner.append(row + [-1] * (SLOT - len(row)))
        index.append(list(members) + [members[-1]] * (most - len(members)))
    owner = jnp.array(owner, jnp.int32)
    keep = owner[:, None, :] == jnp.arange(most, dtype=jnp.int32)[None, :, None]
    rec = jnp.where(keep[:, :, None, None, None, :], rec[:, None], jnp.zeros((), rec.dtype))
    rec = rec.reshape(count, depth, recs * props * SLOT)
    tab = jnp.stack(
        [jnp.concatenate([tables[d] for d in row], axis=-1) for row in index]
    ).reshape(count, radial * dists, depth)

    sums = pl.pallas_call(
        score_kernel,
        grid=(count,),
        in_specs=[
            pl.BlockSpec((1, radial * dists, depth), lambda i: (i, 0, 0)),
            pl.BlockSpec((1, depth, recs * 128), lambda i: (i, 0, 0)),
            pl.BlockSpec((1, half, ligs, 256), lambda i: (i, 0, 0, 0)),
            pl.BlockSpec((1, rots, SLOT, 128), lambda i: (i, 0, 0, 0)),
        ],
        out_specs=pl.BlockSpec((ligs, recs * dists), lambda i: (0, 0)),
        out_shape=jax.ShapeDtypeStruct((ligs, recs * dists), jnp.float32),
        scratch_shapes=[
            pltpu.VMEM((recs * dists, half * 256), jnp.bfloat16),
            pltpu.VMEM((rots * ligs, half * 256), jnp.bfloat16),
            pltpu.VMEM((rots * ligs, recs * dists), jnp.float32),
        ],
        compiler_params=pltpu.CompilerParams(vmem_limit_bytes=48 * 1024 * 1024),
        name="scores",
    )(tab, rec, whole, wig)
    totals = jnp.sum(sums.reshape(ligs, recs, dists), axis=2)
    return jnp.log(totals.T)


def solution(mesh):
    in_specs = (P("rec", None, None), P("rec", None, None), P("rot", None), P(), P())
    out_specs = P("rec", "rot")
    return jax.shard_map(
        per_device, mesh=mesh, in_specs=in_specs, out_specs=out_specs, check_vma=False
    )
```

time: 1410 us -> 189 us (0.13); the launches traced: 1380 us -> 188 us
  local copies, waits for them, and re-layouts: 922 us -> 76.8 us
  matrix products: 412 us -> 0 us
  Pallas kernels: 0 us -> 83.7 us
    reshape x526 -> x1, local copies, waits for them, and re-layouts: 429 us -> 4 us  [per_device(): jnp.transpose(lig, (4, 3, 0, 2, 1, 5))]
    dot_general x502 -> x0, matrix products: 412 us -> none  [the longest x240 256 us: weight_sums(): lax.dot_general(left_part, right_part, (((1,), (1,)), ((), ())), preferre...]
    convert_element_type x243 -> x0, local copies, waits for them, and re-layouts: 228 us -> none  [the longest x232 215 us: rotate_parts(): piece.astype(jnp.bfloat16).reshape(wigner.shape[0] * coeffs.shape[0], -1)]
    slice x264 -> x66, local copies, waits for them, and re-layouts: 211 us -> 36.6 us  [the longest x64 35.1 us: slot_columns(): parts.append(array[..., d * d:d * d + 2 * d + 1])]
    pallas_call x0 -> x2, Pallas kernels: none -> 83.7 us  [the longest x1 66.8 us: per_device(): pl.pallas_call(score_kernel, grid=(count,), in_specs=[pl.BlockSpec((1, ra...]
    all_gather x1 -> x0, local copies, waits for them, and re-layouts: 17.2 us -> none  [per_device(): shard_piece = lax.all_gather(ligands, 'rec', axis=0, tiled=True)]
  transfers between devices with their start and end apart: 1 -> 3, of which waited for: 0 -> 0; matrix products, arithmetic and copies ran while one was open for 10% -> 44% of each run, Pallas kernels for 0% -> 9%
where the time goes in v1:
time: 189 us; the launch traced here: 188 us
  Pallas kernels  83.7 us (44%)
  local copies, waits for them, and re-layouts  76.8 us (41%)
  between operations  13.7 us (7%)
  other arithmetic  7.8 us (4%)
  starting transfers between devices  5.22 us (3%)
    pallas_call x1, Pallas kernels, per_device(): pl.pallas_call(score_kernel, grid=(count,), in_specs=[pl.BlockSpec((1, ra...  66.8 us
    slice x64, local copies, waits for them, and re-layouts, slot_columns(): parts.append(array[..., d * d:d * d + 2 * d + 1])  35.1 us
    pallas_call x1, Pallas kernels, unpack_wigner(): pl.pallas_call(functools.partial(unpack_kernel, groups, front), grid=(row...  17 us
    concatenate x2, local copies, waits for them, and re-layouts, slot_columns(): joined = jnp.concatenate(parts, axis=-1)  8.42 us
    gather x1, local copies, waits for them, and re-layouts, per_device(): tables = jnp.transpose(trans_table[dist_index], (1, 2, 0, 3))  6.61 us
    select_n x1, other arithmetic, per_device(): jnp.where(keep[:, :, None, None, None, :], rec[:, None], jnp.zeros((), re...  6.19 us
    all_to_all x1, starting transfers between devices, per_device(): spread = lax.all_to_all(pieces, 'rec', 0, 0, tiled=False)  5.18 us
    select_n x1, local copies, waits for them, and re-layouts, per_device(): jnp.where(keep[:, :, None, None, None, :], rec[:, None], jnp.zeros((), re...  5.08 us
  transfers between devices with their start and end apart: 3, of which 0 were waited for; matrix products, arithmetic and copies ran while one was open for 44% of the time, Pallas kernels for 9%

profile of v1, /device:TPU:0, one launch (start us, length us, event | category | flops | bytes accessed | tf_op | source)
XLA Modules:
  0.0 188.0 jit_solution(4700804804594258436)
XLA Ops:
  6.5 0.7 all-gather.4.cloned.1.call-update
  7.3 1.0 slice.360
  8.3 1.0 slice.358
  9.3 1.0 slice.357
  10.3 1.0 slice.356
  11.3 1.0 slice.355
  12.7 0.8 slice.350
  13.5 0.8 slice.349
  14.3 0.8 slice.348
  15.0 0.7 slice.347
  15.8 0.8 slice.346
  16.5 0.8 slice.345
  17.3 0.7 slice.344
  18.1 0.8 slice.343
  18.8 0.7 slice.342
  19.6 0.8 slice.341
  20.3 0.8 slice.340
  21.1 0.8 slice.339
  21.8 0.8 slice.338
  22.6 0.8 slice.337
  23.3 0.8 slice.336
  24.1 0.7 slice.335
  24.9 0.8 slice.334
  25.6 0.7 slice.333
  26.4 0.8 slice.361
  27.2 4.1 %concatenate.173 = bf16[8,60,960]{2,0,1:T(8,128)(2,1)S(1)} concatenate(bf16[8,60,59]{2,0,1:T(8,128)(2,1)} %slice.333, bf16[8,60,5]{2,0,1:T(8,128)(2,1)} %slice.334, bf16[8,60,57]{2,0,1:T(8,128)(2,1)} %slice.335, bf16[8,60,7]{2,0,1:T(8,128)(2,1)} %slice.336, bf16[8,60,55]{2,0,1:T(8,128)(2,1)} %slice.337, bf16[8,60,9]{2,0,1:T(8,128)(2,1)} %slice.338, bf16[8,60,53]{2,0,1:T(8,128)(2,1)} %slice.339, ...), dimensions={2} | concatenate | bytes 1843200 | tf_op jit(solution)/shard_map/concatenate | solution.py:45
  31.3 1.4 reshape_reshape.7
  32.8 3.2 %copy.68 = bf16[15,15,8,2,2,64]{5,4,3,2,1,0:T(2,128)(2,1)} copy(bf16[15,15,8,2,2,64]{5,0,2,1,3,4:T(8,128)(2,1)S(1)} %bitcast.81) | data formatting | bytes 1843200 | tf_op jit(solution)/shard_map/transpose | solution.py:158
  36.0 4.0 %reshape.119 = bf16[1800,256]{1,0:T(8,128)(2,1)S(1)} reshape(bf16[15,15,8,2,2,64]{5,4,3,2,1,0:T(2,128)(2,1)} %copy.68) | data formatting | bytes 1843200 | tf_op jit(solution)/shard_map/reshape | solution.py:158
  40.0 1.0 pad.8
  41.1 5.2 %all-to-all-start = ((bf16[8,240,256]{2,1,0:T(8,128)(2,1)}), bf16[8,240,256]{2,1,0:T(8,128)(2,1)}, u32[]{:S(2)}, u32[]{:S(2)}) async-start(bf16[8,240,256]{2,1,0:T(8,128)(2,1)} %bitcast.33), calls=%async_computation | async-start | bytes 1966080 | tf_op jit(solution)/shard_map/all_to_all | solution.py:162
  47.3 0.8 slice.320
  48.0 0.8 slice.319
  48.8 0.8 slice.318
  49.6 0.7 slice.317
  50.3 0.8 slice.316
  51.1 0.8 slice.315
  51.8 0.8 slice.314
  52.6 0.8 slice.313
  53.3 0.7 slice.312
  54.1 0.8 slice.311
  54.8 0.8 slice.310
  55.6 0.8 slice.309
  56.4 0.8 slice.308
  57.1 0.8 slice.307
  57.9 0.8 slice.306
  58.6 0.8 slice.305
  59.4 0.8 slice.304
  60.2 0.8 slice.303
  60.9 0.8 slice.331
  61.7 4.3 %concatenate.172 = bf16[8,60,960]{2,0,1:T(8,128)(2,1)S(1)} concatenate(bf16[8,60,59]{2,0,1:T(8,128)(2,1)} %slice.303, bf16[8,60,5]{2,0,1:T(8,128)(2,1)} %slice.304, bf16[8,60,57]{2,0,1:T(8,128)(2,1)} %slice.305, bf16[8,60,7]{2,0,1:T(8,128)(2,1)} %slice.306, bf16[8,60,55]{2,0,1:T(8,128)(2,1)} %slice.307, bf16[8,60,9]{2,0,1:T(8,128)(2,1)} %slice.308, bf16[8,60,53]{2,0,1:T(8,128)(2,1)} %slice.309, ...), dimensions={2} | concatenate | bytes 1843200 | tf_op jit(solution)/shard_map/concatenate | solution.py:45
  66.0 1.4 reshape_reshape.6
  67.4 3.2 %copy.67 = bf16[15,30,8,2,64]{4,3,2,1,0:T(2,128)(2,1)} copy(bf16[15,30,8,2,64]{4,0,2,1,3:T(8,128)(2,1)S(1)} %bitcast.82) | data formatting | bytes 1843200 | tf_op jit(solution)/shard_map/transpose | solution.py:176
  70.7 1.7 constant_dynamic-slice_fusion
  72.4 6.2 %broadcast_select_fusion = bf16[15,2,30,8,2,64]{5,4,3,2,1,0:T(2,128)(2,1)} fusion(pred[15,2,64]{2,1,0:T(4,128)(4,1)S(1)} %iota_compare_fusion, bf16[15,30,8,2,64]{4,3,2,1,0:T(2,128)(2,1)} %copy.67), kind=kLoop, calls=%fused_computation.1 | loop fusion | flops 921600 | bytes 2766720 | tf_op jit(solution)/shard_map/jit(_where)/select_n | solution.py:188
  78.5 5.1 %select_n.16.rec_ref = bf16[15,60,1024]{2,1,0:T(8,128)(2,1)S(1)} reshape(bf16[15,2,30,8,2,64]{5,4,3,2,1,0:T(2,128)(2,1)} %broadcast_select_fusion) | data formatting | bytes 3686400 | tf_op jit(solution)/shard_map/jit(_where)/select_n | solution.py:188
  83.7 6.6 %gather_fusion = bf16[8,30,30,30]{3,0,2,1:T(8,128)(2,1)} fusion(bf16[16,30,30,30]{3,0,2,1:T(8,128)(2,1)} %param.9, s32[1024]{0:T(1024)S(1)} %pad_clamp_fusion), kind=kCustom, calls=%fused_computation | custom fusion | bytes 864032 | tf_op jit(solution)/shard_map/gather | solution.py:177
  90.3 1.3 slice_bitcast_fusion.19
  93.3 1.8 pad.9.w_ref
  95.1 17.0 %unpack.1.wig_ref = bf16[15,32,64,128]{3,2,1,0:T(8,128)(2,1)} custom-call(bf16[32,36480]{1,0:T(8,128)(2,1)S(1)} %pad.9.w_ref), custom_call_target="tpu_custom_call" | custom-call | tf_op jit(solution)/shard_map/unpack/pallas_call | solution.py:77
  112.1 1.5 slice-done.4
  113.6 0.1 copy.72
  113.7 66.8 %scores.1 = f32[16,64]{1,0:T(8,128)S(1)} custom-call(bf16[15,240,60]{2,1,0:T(8,128)(2,1)S(1)} %maximum_dynamic-update-slice_fusion.tab_ref, bf16[15,60,1024]{2,1,0:T(8,128)(2,1)S(1)} %select_n.16.rec_ref, bf16[15,15,16,256]{3,2,1,0:T(8,128)(2,1)S(1)} %bitcast.78, bf16[15,32,64,128]{3,2,1,0:T(8,128)(2,1)} %unpack.1.wig_ref), custom_call_target="tpu_custom_call" | custom-call | tf_op jit(solution)/shard_map/scores/pallas_call | solution.py:194
  180.6 0.6 log_bitcast_fusion
  (60 shorter events, 3.3 us)
Async XLA Ops:
  6.5 5.8 %copy-start = (bf16[8,60,900]{2,0,1:T(8,128)(2,1)S(1)}, bf16[8,60,900]{2,0,1:T(8,128)(2,1)}, u32[]{:S(2)}) copy-start(bf16[8,60,900]{2,0,1:T(8,128)(2,1)} %param.7) | copy-start | bytes 2592004
  6.5 86.8 %all-gather.4.cloned.1.call-start = ((), (), s32[]{:S(2)}) async-start(), calls=%async_computation.1 | async-start | bytes 2887680 | tf_op jit(solution)/shard_map/all_gather | solution.py:169
  16.5 10.6 %slice-start = ((bf16[8,60,900]{2,0,1:T(8,128)(2,1)}), bf16[8,60,33]{2,0,1:T(8,128)(2,1)S(1)}, s32[]{:S(2)}) async-start(bf16[8,60,900]{2,0,1:T(8,128)(2,1)} %param.7), calls=%async_computation.3 | async-start | bytes 245760 | tf_op jit(solution)/shard_map/slice | solution.py:41
  16.5 10.6 %slice-start.1 = ((bf16[8,60,900]{2,0,1:T(8,128)(2,1)}), bf16[8,60,1]{2,0,1:T(8,128)(2,1)S(1)}, s32[]{:S(2)}) async-start(bf16[8,60,900]{2,0,1:T(8,128)(2,1)} %param.7), calls=%async_computation.4 | async-start | bytes 245760 | tf_op jit(solution)/shard_map/slice | solution.py:41
  40.0 6.3 %copy-start.1 = (bf16[8,60,900]{2,0,1:T(8,128)(2,1)S(1)}, bf16[8,60,900]{2,0,1:T(8,128)(2,1)}, u32[]{:S(2)}) copy-start(bf16[8,60,900]{2,0,1:T(8,128)(2,1)} %param.6) | copy-start | bytes 2592004
  41.1 29.6 %all-to-all-start = ((bf16[8,240,256]{2,1,0:T(8,128)(2,1)}), bf16[8,240,256]{2,1,0:T(8,128)(2,1)}, u32[]{:S(2)}, u32[]{:S(2)}) async-start(bf16[8,240,256]{2,1,0:T(8,128)(2,1)} %bitcast.33), calls=%async_computation | async-start | bytes 1966080 | tf_op jit(solution)/shard_map/all_to_all | solution.py:162
  46.2 65.8 %all-gather.6.cloned.1.call-start = ((), (), s32[]{:S(2)}) async-start(), calls=%async_computation.2 | async-start | bytes 2211840 | tf_op jit(solution)/shard_map/all_gather | solution.py:164
  50.3 11.4 %slice-start.2 = ((bf16[8,60,900]{2,0,1:T(8,128)(2,1)}), bf16[8,60,33]{2,0,1:T(8,128)(2,1)S(1)}, s32[]{:S(2)}) async-start(bf16[8,60,900]{2,0,1:T(8,128)(2,1)} %param.6), calls=%async_computation.5 | async-start | bytes 245760 | tf_op jit(solution)/shard_map/slice | solution.py:41
  50.3 11.4 %slice-start.3 = ((bf16[8,60,900]{2,0,1:T(8,128)(2,1)}), bf16[8,60,1]{2,0,1:T(8,128)(2,1)S(1)}, s32[]{:S(2)}) async-start(bf16[8,60,900]{2,0,1:T(8,128)(2,1)} %param.6), calls=%async_computation.6 | async-start | bytes 245760 | tf_op jit(solution)/shard_map/slice | solution.py:41
  67.4 3.2 %copy-start.3 = (s32[15,64]{1,0:T(8,128)S(1)}, s32[15,64]{1,0:T(8,128)}, u32[]{:S(2)}) copy-start(s32[15,64]{1,0:T(8,128)} %constant.7.clone) | copy-start | bytes 11524
  78.5 5.1 %copy-start.4 = (s32[8]{0:T(128)S(1)}, s32[8]{0:T(128)}, u32[]{:S(2)}) copy-start(s32[8]{0:T(128)} %param.10) | copy-start | bytes 100
  90.3 1.8 copy-start.2
  112.1 1.5 slice-start.4
Sparse Core Ops, SparseCore 0:
  8.9 52.3 all-gather.3
  72.5 29.4 all-gather.5

commit v2 on v1

v2 whole, which is shorter than its diff:
```python
import functools
import math

import jax
import jax.numpy as jnp
from jax import lax
from jax.experimental import pallas as pl
from jax.experimental.pallas import tpu as pltpu
from jax.sharding import PartitionSpec as P

SLOT = 64


def packed_start(degree):
    return degree * (4 * degree * degree - 1) // 3


def degree_groups(degrees):
    left = list(range(degrees))
    groups = []
    while left:
        members = [left.pop()]
        used = 2 * members[0] + 1
        while left:
            fits = [d for d in left if used + 2 * d + 1 <= SLOT]
            if not fits:
                break
            pick = fits[-1]
            left.remove(pick)
            members.append(pick)
            used += 2 * pick + 1
        groups.append(members)
    return groups


def column_sources(groups):
    sources = []
    for members in groups + [[]] * (len(groups) % 2):
        row = []
        for d in members:
            row += range(d * d, d * d + 2 * d + 1)
        sources += row + [-1] * (SLOT - len(row))
    return jnp.array(sources, jnp.int32)[None, :]


def select_columns(source, rows):
    shape = (rows.shape[-1], source.shape[1])
    hit = lax.broadcasted_iota(jnp.int32, shape, 0) == source
    return jnp.dot(
        rows, jnp.where(hit, 1.0, 0.0).astype(jnp.bfloat16), preferred_element_type=jnp.float32
    )


def merge_slots(first, second, group):
    lo = group // 2 * 128
    first = first[:, lo : lo + 128]
    second = second[:, lo : lo + 128]
    lane = lax.broadcasted_iota(jnp.int32, first.shape, 1)
    if group % 2:
        return jnp.where(lane < SLOT, pltpu.roll(first, SLOT, 1), second)
    return jnp.where(lane < SLOT, first, pltpu.roll(second, SLOT, 1))


def ligand_kernel(source_ref, lig_ref, out_ref):
    count, rows, _ = out_ref.shape
    slots = select_columns(source_ref[...], lig_ref[...])
    for group in range(count):
        for half in range(2):
            first = slots[half * 2 * rows : (half * 2 + 1) * rows]
            second = slots[(half * 2 + 1) * rows : (half * 2 + 2) * rows]
            merged = merge_slots(first, second, group)
            out_ref[group, :, half * 128 : (half + 1) * 128] = merged.astype(jnp.bfloat16)


def receptor_kernel(groups, depth, source_ref, rec_ref, out_ref):
    slots = select_columns(source_ref[...], rec_ref[...])
    recs = out_ref.shape[2] // 128
    lane = lax.broadcasted_iota(jnp.int32, (depth, 128), 1) % SLOT
    for group, members in enumerate(groups):
        split = 2 * members[0] + 1
        for r in range(recs):
            first = slots[2 * r * depth : (2 * r + 1) * depth]
            second = slots[(2 * r + 1) * depth : (2 * r + 2) * depth]
            merged = merge_slots(first, second, group)
            both = jnp.concatenate(
                [jnp.where(lane < split, merged, 0.0), jnp.where(lane < split, 0.0, merged)], axis=0
            )
            out_ref[group, :, r * 128 : (r + 1) * 128] = both.astype(jnp.bfloat16)


def unpack_kernel(groups, front, w_ref, out_ref, scr):
    rows = w_ref.shape[0]
    lane = lax.broadcasted_iota(jnp.int32, (rows, 128), 1)
    for index, members in enumerate(groups):
        used = 0
        for d in members:
            extent = 2 * d + 1
            keep = (lane >= used) & (lane < used + extent)
            for m in range(extent):
                start = front + packed_start(d) + m * extent - used
                base = start // 128 * 128
                window = w_ref[:, base : base + 256].astype(jnp.float32)
                shift = start - base
                if shift:
                    window = pltpu.roll(window, 256 - shift, 1)
                scr[:, used + m, :] = jnp.where(keep, window[:, :128], 0.0)
            used += extent
        for m in range(used, SLOT):
            scr[:, m, :] = jnp.zeros((rows, 128), jnp.float32)
        out_ref[index] = scr[...].astype(jnp.bfloat16)


def unpack_wigner(wigner, groups):
    front = 128
    rows, width = wigner.shape
    total = (front + width + 127) // 128 * 128 + 256
    padded = jnp.pad(wigner, ((0, 0), (front, total - front - width)))
    qstep = 8 if rows % 16 else 16
    return pl.pallas_call(
        functools.partial(unpack_kernel, groups, front),
        grid=(rows // qstep,),
        in_specs=[pl.BlockSpec((qstep, total), lambda i: (i, 0))],
        out_specs=pl.BlockSpec((len(groups), qstep, SLOT, 128), lambda i: (0, i, 0, 0)),
        out_shape=jax.ShapeDtypeStruct((len(groups), rows, SLOT, 128), jnp.bfloat16),
        scratch_shapes=[pltpu.VMEM((qstep, SLOT, 128), jnp.float32)],
        compiler_params=pltpu.CompilerParams(vmem_limit_bytes=48 * 1024 * 1024),
        name="unpack",
    )(padded)


def score_kernel(
    tab_ref, rec_ref, lig_a_ref, lig_b_ref, wig_a_ref, wig_b_ref, out_ref, trans, rot, acc
):
    step = pl.program_id(0)
    rots = wig_a_ref.shape[1]
    recs = rec_ref.shape[2] // 128
    rad = trans.shape[1] // 256
    dists = tab_ref.shape[1] // (2 * rad)
    part = lig_a_ref.shape[1] // rad
    ligs = 2 * part

    @pl.when(step == 0)
    def _():
        acc[...] = jnp.zeros_like(acc)

    moved = jnp.dot(tab_ref[0], rec_ref[0], preferred_element_type=jnp.float32)
    moved = moved.reshape(2, rad, dists, recs * 128)
    for xq in range(rad):
        for half in range(2):
            piece = jnp.concatenate(
                [moved[half, xq, :, r * 128 : (r + 1) * 128] for r in range(recs)], axis=0
            )
            lo = xq * 256 + half * 128
            trans[:, lo : lo + 128] = piece.astype(jnp.bfloat16)

    low = lig_a_ref[0].astype(jnp.float32)
    high = lig_b_ref[0].astype(jnp.float32)
    rows = []
    for xq in range(rad):
        rows.append(low[xq * part : (xq + 1) * part])
        rows.append(high[xq * part : (xq + 1) * part])
    coeffs = jnp.concatenate(rows, axis=0).astype(jnp.bfloat16)
    none = jnp.zeros((2 * SLOT, 128), jnp.bfloat16)

    for source, wig_ref in enumerate((wig_a_ref, wig_b_ref)):

        def one_rotation(q, carry, wig_ref=wig_ref, source=source):
            block = wig_ref[0, q]
            other = pltpu.roll(block.astype(jnp.float32), SLOT, 1).astype(jnp.bfloat16)
            pair = jnp.concatenate([block, other], axis=0)
            full = jnp.concatenate(
                [jnp.concatenate([pair, none], axis=1), jnp.concatenate([none, pair], axis=1)],
                axis=0,
            )
            turned = jnp.dot(coeffs, full, preferred_element_type=jnp.float32).astype(jnp.bfloat16)
            row = pl.multiple_of((q + source * rots) * ligs, 16)
            for xq in range(rad):
                rot[pl.ds(row, ligs), xq * 256 : (xq + 1) * 256] = turned[
                    xq * ligs : (xq + 1) * ligs
                ]
            return carry

        lax.fori_loop(0, rots, one_rotation, 0, unroll=4)

    acc[...] += lax.dot_general(
        rot[...], trans[...], (((1,), (1,)), ((), ())), preferred_element_type=jnp.float32
    )

    @pl.when(step == pl.num_programs(0) - 1)
    def _():
        weights = jnp.exp(acc[...])
        out_ref[...] = jnp.sum(weights.reshape(2 * rots, ligs, acc.shape[1]), axis=0)


def per_device(receptors, ligands, wigner, trans_table, dist_index):
    degrees = trans_table.shape[1]
    radial = trans_table.shape[2]
    half = radial // 2
    groups = degree_groups(degrees)
    count = len(groups)
    padded = count + count % 2
    source = column_sources(groups)
    recs, rows, angular = receptors.shape
    props = rows // radial
    dists = dist_index.shape[0]
    nrec = lax.axis_size("rec")
    part = ligands.shape[0]
    ligs = 2 * part
    params = pltpu.CompilerParams(vmem_limit_bytes=48 * 1024 * 1024)
    core = lax.axis_index("rec") % 2
    swap = [(i, i ^ 1) for i in range(nrec)]
    same_core = [list(range(c, nrec, 2)) for c in range(2)]

    share = wigner.shape[0] // 2
    own = lax.dynamic_slice_in_dim(wigner, core * share, share, 0)
    turns_a = lax.all_gather(own, "rot", axis=0, tiled=True)
    turns_b = lax.ppermute(turns_a, "rec", swap)
    rots = turns_a.shape[0]

    lig = ligands.reshape(part, props, 2, half, angular)
    lig = jnp.transpose(lig, (2, 1, 3, 0, 4)).reshape(4 * half * part, angular)
    lig = pl.pallas_call(
        ligand_kernel,
        out_shape=jax.ShapeDtypeStruct((padded, half * part, 256), jnp.bfloat16),
        compiler_params=params,
        name="ligand_slots",
    )(source, lig)
    pieces = lig.reshape(nrec // 2, -1, 256)
    spread = lax.all_to_all(pieces, "rec", 0, 0, axis_index_groups=same_core)
    mine = lax.dynamic_index_in_dim(spread, lax.axis_index("rot"), 0, keepdims=False)
    lig_a = lax.all_gather(mine, "rec", axis=0, axis_index_groups=same_core)
    lig_b = lax.ppermute(lig_a, "rec", swap)
    lig_a = lig_a.reshape(padded, half * part, 256)
    lig_b = lig_b.reshape(padded, half * part, 256)

    wig_a = unpack_wigner(turns_a, groups)
    wig_b = unpack_wigner(turns_b, groups)

    deep = (radial + 15) // 16 * 16
    rec = receptors.reshape(recs * props, radial, angular)
    rec = jnp.pad(rec, ((0, 0), (0, deep - radial), (0, 0))).reshape(-1, angular)
    rec = pl.pallas_call(
        functools.partial(receptor_kernel, groups, deep),
        out_shape=jax.ShapeDtypeStruct((count, 2 * deep, recs * 128), jnp.bfloat16),
        compiler_params=params,
        name="receptor_slots",
    )(source, rec)
    tables = jnp.transpose(trans_table[dist_index], (1, 2, 0, 3))
    tables = jnp.pad(tables, ((0, 0), (0, 0), (0, 0), (0, deep - radial)))
    tab = jnp.stack([jnp.concatenate([tables[d] for d in row], axis=-1) for row in groups])
    tab = tab.reshape(count, radial * dists, 2 * deep)

    sums = pl.pallas_call(
        score_kernel,
        grid=(count,),
        in_specs=[
            pl.BlockSpec((1, radial * dists, 2 * deep), lambda i: (i, 0, 0)),
            pl.BlockSpec((1, 2 * deep, recs * 128), lambda i: (i, 0, 0)),
            pl.BlockSpec((1, half * part, 256), lambda i: (i, 0, 0)),
            pl.BlockSpec((1, half * part, 256), lambda i: (i, 0, 0)),
            pl.BlockSpec((1, rots, SLOT, 128), lambda i: (i, 0, 0, 0)),
            pl.BlockSpec((1, rots, SLOT, 128), lambda i: (i, 0, 0, 0)),
        ],
        out_specs=pl.BlockSpec((ligs, recs * dists), lambda i: (0, 0)),
        out_shape=jax.ShapeDtypeStruct((ligs, recs * dists), jnp.float32),
        scratch_shapes=[
            pltpu.VMEM((recs * dists, half * 256), jnp.bfloat16),
            pltpu.VMEM((2 * rots * ligs, half * 256), jnp.bfloat16),
            pltpu.VMEM((2 * rots * ligs, recs * dists), jnp.float32),
        ],
        compiler_params=params,
        name="scores",
    )(tab, rec, lig_a, lig_b, wig_a, wig_b)
    totals = jnp.sum(sums.reshape(2, part, recs, dists), axis=3)
    totals = jnp.where(core == 0, totals, totals[::-1]).reshape(ligs, recs)
    return jnp.log(totals.T)


def solution(mesh):
    in_specs = (P("rec", None, None), P("rec", None, None), P("rot", None), P(), P())
    out_specs = P("rec", "rot")
    return jax.shard_map(
        per_device, mesh=mesh, in_specs=in_specs, out_specs=out_specs, check_vma=False
    )
```

time: 189 us -> 158 us (0.84)
  local copies, waits for them, and re-layouts: 76.8 us -> 27.3 us
  blocking collectives: 0 us -> 15.2 us
    slice x66 -> x0, local copies, waits for them, and re-layouts: 36.6 us -> none  [the longest x64 35.1 us: slot_columns(): parts.append(array[..., d * d:d * d + 2 * d + 1])]
    all_gather x0 -> x1, blocking collectives: none -> 15.2 us  [per_device(): lig_a = lax.all_gather(mine, 'rec', axis=0, axis_index_groups=same_core)]
    unnamed x10 -> x37, local copies, waits for them, and re-layouts: 0.02 us -> 10.8 us
    concatenate x2 -> x0, local copies, waits for them, and re-layouts: 8.42 us -> none  [slot_columns(): joined = jnp.concatenate(parts, axis=-1)]
    unnamed x14, other arithmetic: 1.47 us -> 8.35 us
    transpose x3 -> x0, local copies, waits for them, and re-layouts: 6.58 us -> none  [the longest x1 3.23 us: per_device(): jnp.transpose(lig, (4, 3, 0, 2, 1, 5))]
    select_n x1 -> x0, other arithmetic: 6.19 us -> none  [per_device(): jnp.where(keep[:, :, None, None, None, :], rec[:, None], jnp.zeros((), re...]
    select_n x1 -> x0, local copies, waits for them, and re-layouts: 5.08 us -> none  [per_device(): jnp.where(keep[:, :, None, None, None, :], rec[:, None], jnp.zeros((), re...]
  transfers between devices with their start and end apart: 3 -> 4, of which waited for: 0 -> 1; matrix products, arithmetic and copies ran while one was open for 44% -> 17% of each run, Pallas kernels for 9% -> 12%
where the time goes in v2:
time: 158 us; the launch traced here: 157 us
  Pallas kernels  85.3 us (54%)
  local copies, waits for them, and re-layouts  27.3 us (17%)
  blocking collectives  15.2 us (10%)
  between operations  13.7 us (9%)
  other arithmetic  8.57 us (5%)
  starting transfers between devices  5.24 us (3%)
    pallas_call x1, Pallas kernels, per_device(): pl.pallas_call(score_kernel, grid=(count,), in_specs=[pl.BlockSpec((1, ra...  66.6 us
    all_gather x1, blocking collectives, per_device(): lig_a = lax.all_gather(mine, 'rec', axis=0, axis_index_groups=same_core)  15.2 us
    pallas_call x2, Pallas kernels, unpack_wigner(): pl.pallas_call(functools.partial(unpack_kernel, groups, front), grid=(row...  14.8 us
    unnamed x37, local copies, waits for them, and re-layouts  10.8 us
    unnamed x14, other arithmetic  8.35 us
    gather x1, local copies, waits for them, and re-layouts, per_device(): tables = jnp.transpose(trans_table[dist_index], (1, 2, 0, 3))  5.68 us
    all_to_all x1, starting transfers between devices, per_device(): spread = lax.all_to_all(pieces, 'rec', 0, 0, axis_index_groups=same_core)  5.16 us
    concatenate x2, local copies, waits for them, and re-layouts, per_device(): jnp.concatenate([tables[d] for d in row], axis=-1)  3.37 us
  transfers between devices with their start and end apart: 4, of which 1 were waited for; matrix products, arithmetic and copies ran while one was open for 17% of the time, Pallas kernels for 12%

profile of v2, /device:TPU:0, one launch (start us, length us, event | category | flops | bytes accessed | tf_op | source)
XLA Modules:
  0.0 156.6 jit_solution(10481984896788410527)
XLA Ops:
  6.5 0.0 copy-start
  6.5 0.0 all-gather.3.cloned.1.call-start
  6.5 1.1 copy-done
  7.6 0.9 dynamic-slice_bitcast_fusion
  8.4 0.0 all-gather.3.cloned.1.call-update
  8.5 1.3 copy.11
  9.8 0.0 copy-done.3
  9.8 0.0 copy-start.16
  9.8 2.3 %ligand_slots.1 = bf16[16,120,256]{2,1,0:T(8,128)(2,1)} custom-call(s32[1,1024]{1,0:T(1,128)S(1)} %copy-done.3, bf16[480,900]{1,0:T(8,128)(2,1)S(1)} %bitcast.76), custom_call_target="tpu_custom_call" | custom-call | tf_op jit(solution)/shard_map/ligand_slots/pallas_call | solution.py:222
  12.1 5.2 %all-to-all-start = ((bf16[4,480,256]{2,1,0:T(8,128)(2,1)}), bf16[4,480,256]{2,1,0:T(8,128)(2,1)}, u32[]{:S(2)}, u32[]{:S(2)}) async-start(bf16[4,480,256]{2,1,0:T(8,128)(2,1)} %bitcast.35), calls=%async_computation | async-start | bytes 1966080 | tf_op jit(solution)/shard_map/all_to_all | solution.py:229
  17.3 0.0 copy-done.16
  17.3 5.7 %gather_fusion = bf16[8,30,30,30]{3,0,2,1:T(8,128)(2,1)S(1)} fusion(bf16[16,30,30,30]{3,0,2,1:T(8,128)(2,1)} %param.9, s32[1024]{0:T(1024)S(1)} %pad_clamp_fusion), kind=kCustom, calls=%fused_computation | custom fusion | bytes 864032 | tf_op jit(solution)/shard_map/gather | solution.py:248
  23.0 0.0 copy-start.4
  23.0 1.0 slice_bitcast_fusion.19
  24.0 0.1 maximum_dynamic-update-slice_fusion.14
  24.1 2.7 %copy.10 = bf16[8,60,900]{2,1,0:T(8,128)(2,1)} copy(bf16[8,60,900]{2,0,1:T(8,128)(2,1)} %param.6) | data formatting | bytes 1728000 | tf_op args[0]
  26.8 0.0 copy-done.4
  26.8 2.3 %reshape.117 = bf16[16,30,900]{2,1,0:T(8,128)(2,1)} reshape(bf16[8,60,900]{2,1,0:T(8,128)(2,1)} %copy.10) | data formatting | bytes 1728000 | tf_op jit(solution)/shard_map/reshape | solution.py:240
  29.1 1.4 pad.16
  30.5 1.6 %receptor_slots.1.rec_ref = bf16[15,64,1024]{2,1,0:T(8,128)(2,1)S(1)} custom-call(s32[1,1024]{1,0:T(1,128)S(1)} %copy-done.3, bf16[512,900]{1,0:T(8,128)(2,1)S(1)} %bitcast.74), custom_call_target="tpu_custom_call" | custom-call | tf_op jit(solution)/shard_map/receptor_slots/pallas_call | solution.py:242
  32.1 1.0 maximum_dynamic-update-slice_fusion.13
  33.0 1.0 maximum_dynamic-update-slice_fusion.12
  34.0 1.0 maximum_dynamic-update-slice_fusion.11
  35.0 1.0 maximum_dynamic-update-slice_fusion.10
  35.9 2.4 %slice_bitcast_fusion.1 = (bf16[1,240,32]{2,1,0:T(8,128)(2,1)}, bf16[1,240,32]{2,1,0:T(8,128)(2,1)}, bf16[1,240,32]{2,1,0:T(8,128)(2,1)}, bf16[1,240,32]{2,1,0:T...) fusion(bf16[30,30,8,30]{3,2,1,0:T(8,128)(2,1)} %bitcast.79), kind=kLoop, calls=%fused_computation.18 | loop fusion | bytes 723840 | tf_op jit(solution)/shard_map/concatenate | solution.py:250
  38.3 0.1 maximum_dynamic-update-slice_fusion.9
  38.4 0.0 all-to-all-done
  38.4 1.7 %constant_dynamic-slice_fusion = bf16[1,480,256]{2,1,0:T(8,128)(2,1)} fusion(bf16[4,480,256]{2,1,0:T(8,128)(2,1)} %all-to-all-done, s32[]{:T(128)S(6)} %select_n.28), kind=kLoop, calls=%fused_computation.52 | loop fusion | bytes 491524 | tf_op jit(solution)/shard_map/jit(dynamic_index_in_dim)/dynamic_slice | solution.py:230
  40.1 1.3 all-gather.3.cloned.1.call-done
  41.4 2.4 %reshape.135 = bf16[16,35990]{1,0:T(8,128)(2,1)} reshape(bf16[4,4,35990]{2,1,0:T(4,128)(2,1)} %all-gather.3.cloned.1.call-done) | data formatting | bytes 2303360
  43.7 0.0 copy-start.11
  43.7 0.0 copy-start.8
  43.7 0.0 copy-start.9
  43.7 0.0 copy-start.6
  43.8 0.0 copy-start.7
  43.8 0.0 copy-start.5
  43.8 0.1 collective-permute-start.1
  43.9 15.2 %all_gather.7 = bf16[4,480,256]{2,1,0:T(8,128)(2,1)S(1)} all-gather(bf16[1,480,256]{2,1,0:T(8,128)(2,1)} %constant_dynamic-slice_fusion), channel_id=1, replica_groups={{0,8,16,24},{4,12,20,28},{1,9,17,25},{5,13,21,29},{2,10,18,26},{6,14,22..., dimensions={0}, use_global_device_ids=true | all-gather | bytes 1228800 | tf_op jit(solution)/shard_map/all_gather | solution.py:231
  59.1 0.0 collective-permute-start
  59.1 1.0 maximum_dynamic-update-slice_fusion.8
  60.1 1.0 maximum_dynamic-update-slice_fusion.7
  61.0 1.0 maximum_dynamic-update-slice_fusion.6
  62.0 1.0 maximum_dynamic-update-slice_fusion.5
  63.0 0.0 copy-done.14
  63.0 0.0 copy-done.15
  63.0 0.1 maximum_dynamic-update-slice_fusion.4
  63.1 0.0 copy-done.13
  63.1 0.1 maximum_dynamic-update-slice_fusion.3
  63.2 0.1 maximum_dynamic-update-slice_fusion.2
  63.3 0.1 maximum_dynamic-update-slice_fusion.1
  63.5 0.0 copy-done.6
  63.5 0.1 maximum_dynamic-update-slice_fusion.tab_ref
  63.6 0.1 pad.17.w_ref
  63.7 7.4 %unpack.2.wig_a_ref = bf16[15,16,64,128]{3,2,1,0:T(8,128)(2,1)S(1)} custom-call(bf16[16,36480]{1,0:T(8,128)(2,1)S(1)} %pad.17.w_ref), custom_call_target="tpu_custom_call" | custom-call | tf_op jit(solution)/shard_map/unpack/pallas_call | solution.py:119
  71.1 1.9 %copy-done.1 = bf16[15,16,64,128]{3,2,1,0:T(8,128)(2,1)} copy-done((bf16[15,16,64,128]{3,2,1,0:T(8,128)(2,1)}, bf16[15,16,64,128]{3,2,1,0:T(8,128)(2,1)S(1)}, u32[]{:S(2)}) %copy-start.1) | copy-done | bytes 3932184
  72.9 0.0 collective-permute-done.1
  72.9 0.1 pad.18.w_ref
  73.0 7.4 %unpack.3.wig_b_ref = bf16[15,16,64,128]{3,2,1,0:T(8,128)(2,1)S(1)} custom-call(bf16[16,36480]{1,0:T(8,128)(2,1)S(1)} %pad.18.w_ref), custom_call_target="tpu_custom_call" | custom-call | tf_op jit(solution)/shard_map/unpack/pallas_call | solution.py:119
  80.4 1.9 %copy-done.2 = bf16[15,16,64,128]{3,2,1,0:T(8,128)(2,1)} copy-done((bf16[15,16,64,128]{3,2,1,0:T(8,128)(2,1)}, bf16[15,16,64,128]{3,2,1,0:T(8,128)(2,1)S(1)}, u32[]{:S(2)}) %copy-start.2) | copy-done | bytes 3932184
  82.3 0.0 collective-permute-done
  82.3 66.6 %scores.1 = f32[16,64]{1,0:T(8,128)S(1)} custom-call(bf16[15,240,64]{2,1,0:T(8,128)(2,1)S(1)} %maximum_dynamic-update-slice_fusion.tab_ref, bf16[15,64,1024]{2,1,0:T(8,128)(2,1)S(1)} %receptor_slots.1.rec_ref, bf16[16,120,256]{2,1,0:T(8,128)(2,1)S(1)} %bitcast.75, bf16[16,120,256]{2,1,0:T(8,128)(2,1)S(1)} %bitcast.77, bf16[15,16,64,128]{3,2,1,0:T(8,128)(2,1)} %copy-done.1, ...), custom_call_target="tpu_custom_call" | custom-call | tf_op jit(solution)/shard_map/scores/pallas_call | solution.py:253
  148.9 0.1 reshape.124
  149.0 0.1 reduce_sum.9
  149.1 0.7 copy.13
  (18 shorter events, 0.0 us)
Async XLA Ops:
  6.5 1.1 copy-start
  6.5 3.2 %copy-start.3 = (s32[1,1024]{1,0:T(1,128)S(1)}, s32[1,1024]{1,0:T(1,128)}, u32[]{:S(2)}) copy-start(s32[1,1024]{1,0:T(1,128)} %constant.49.source_ref) | copy-start | bytes 12292
  6.5 34.8 %all-gather.3.cloned.1.call-start = ((), (), s32[]{:S(2)}) async-start(), calls=%async_computation.1 | async-start | bytes 1443840 | tf_op jit(solution)/shard_map/all_gather | solution.py:216
  9.8 7.5 %copy-start.16 = (s32[8]{0:T(128)S(1)}, s32[8]{0:T(128)}, u32[]{:S(2)}) copy-start(s32[8]{0:T(128)} %param.10) | copy-start | bytes 100
  12.1 26.3 %all-to-all-start = ((bf16[4,480,256]{2,1,0:T(8,128)(2,1)}), bf16[4,480,256]{2,1,0:T(8,128)(2,1)}, u32[]{:S(2)}, u32[]{:S(2)}) async-start(bf16[4,480,256]{2,1,0:T(8,128)(2,1)} %bitcast.35), calls=%async_computation | async-start | bytes 1966080 | tf_op jit(solution)/shard_map/all_to_all | solution.py:229
  23.0 3.9 %copy-start.4 = (bf16[8,30,30,30]{3,0,2,1:T(8,128)(2,1)}, bf16[8,30,30,30]{3,0,2,1:T(8,128)(2,1)S(1)}, u32[]{:S(2)}) copy-start(bf16[8,30,30,30]{3,0,2,1:T(8,128)(2,1)S(1)} %gather_fusion) | copy-start | bytes 1296004
  40.1 23.1 %copy-start.10 = (bf16[1,240,32]{2,1,0:T(8,128)(2,1)S(1)}, bf16[1,240,32]{2,1,0:T(8,128)(2,1)}, u32[]{:S(2)}) copy-start(bf16[1,240,32]{2,1,0:T(8,128)(2,1)} %get-tuple-element.9) | copy-start | bytes 46084
  43.7 19.2 %copy-start.14 = (bf16[1,240,32]{2,1,0:T(8,128)(2,1)S(1)}, bf16[1,240,32]{2,1,0:T(8,128)(2,1)}, u32[]{:S(2)}) copy-start(bf16[1,240,32]{2,1,0:T(8,128)(2,1)} %get-tuple-element.13) | copy-start | bytes 46084
  43.7 19.3 %copy-start.15 = (bf16[1,240,32]{2,1,0:T(8,128)(2,1)S(1)}, bf16[1,240,32]{2,1,0:T(8,128)(2,1)}, u32[]{:S(2)}) copy-start(bf16[1,240,32]{2,1,0:T(8,128)(2,1)} %get-tuple-element.14) | copy-start | bytes 46084
  43.7 19.4 %copy-start.12 = (bf16[1,240,32]{2,1,0:T(8,128)(2,1)S(1)}, bf16[1,240,32]{2,1,0:T(8,128)(2,1)}, u32[]{:S(2)}) copy-start(bf16[1,240,32]{2,1,0:T(8,128)(2,1)} %get-tuple-element.11) | copy-start | bytes 46084
  43.7 19.4 %copy-start.13 = (bf16[1,240,32]{2,1,0:T(8,128)(2,1)S(1)}, bf16[1,240,32]{2,1,0:T(8,128)(2,1)}, u32[]{:S(2)}) copy-start(bf16[1,240,32]{2,1,0:T(8,128)(2,1)} %get-tuple-element.12) | copy-start | bytes 46084
  43.7 19.5 %copy-start.11 = (bf16[1,240,32]{2,1,0:T(8,128)(2,1)S(1)}, bf16[1,240,32]{2,1,0:T(8,128)(2,1)}, u32[]{:S(2)}) copy-start(bf16[1,240,32]{2,1,0:T(8,128)(2,1)} %get-tuple-element.10) | copy-start | bytes 46084
  43.7 19.6 %copy-start.8 = (bf16[1,240,32]{2,1,0:T(8,128)(2,1)S(1)}, bf16[1,240,32]{2,1,0:T(8,128)(2,1)}, u32[]{:S(2)}) copy-start(bf16[1,240,32]{2,1,0:T(8,128)(2,1)} %get-tuple-element.7) | copy-start | bytes 46084
  43.7 19.6 %copy-start.9 = (bf16[1,240,32]{2,1,0:T(8,128)(2,1)S(1)}, bf16[1,240,32]{2,1,0:T(8,128)(2,1)}, u32[]{:S(2)}) copy-start(bf16[1,240,32]{2,1,0:T(8,128)(2,1)} %get-tuple-element.8) | copy-start | bytes 46084
  43.7 19.7 %copy-start.6 = (bf16[1,240,32]{2,1,0:T(8,128)(2,1)S(1)}, bf16[1,240,32]{2,1,0:T(8,128)(2,1)}, u32[]{:S(2)}) copy-start(bf16[1,240,32]{2,1,0:T(8,128)(2,1)} %get-tuple-element.5) | copy-start | bytes 46084
  43.8 19.7 %copy-start.7 = (bf16[1,240,32]{2,1,0:T(8,128)(2,1)S(1)}, bf16[1,240,32]{2,1,0:T(8,128)(2,1)}, u32[]{:S(2)}) copy-start(bf16[1,240,32]{2,1,0:T(8,128)(2,1)} %get-tuple-element.6) | copy-start | bytes 46084
  43.8 19.8 %copy-start.5 = (bf16[16,35990]{1,0:T(8,128)(2,1)S(1)}, bf16[16,35990]{1,0:T(8,128)(2,1)}, u32[]{:S(2)}) copy-start(bf16[16,35990]{1,0:T(8,128)(2,1)} %reshape.135) | copy-start | bytes 3455044
  43.8 29.1 %collective-permute-start.1 = (bf16[16,35990]{1,0:T(8,128)(2,1)}, bf16[16,35990]{1,0:T(8,128)(2,1)S(1)}, u32[]{:S(2)}, u32[]{:S(2)}) collective-permute-start(bf16[16,35990]{1,0:T(8,128)(2,1)} %reshape.135), channel_id=1, source_target_pairs={{0,4},{4,0},{8,12},{12,8},{16,20},{20,16},{24,28},{28,24},{1,5},{5... | collective-permute-start | bytes 3455048 | tf_op jit(solution)/shard_map/ppermute | solution.py:217
  59.1 23.2 %collective-permute-start = (bf16[4,480,256]{2,1,0:T(8,128)(2,1)S(1)}, bf16[4,480,256]{2,1,0:T(8,128)(2,1)S(1)}, u32[]{:S(2)}, u32[]{:S(2)}) collective-permute-start(bf16[4,480,256]{2,1,0:T(8,128)(2,1)S(1)} %all_gather.7), channel_id=1, source_target_pairs={{0,4},{4,0},{8,12},{12,8},{16,20},{20,16},{24,28},{28,24},{1,5},{5... | collective-permute-start | bytes 2949128 | tf_op jit(solution)/shard_map/ppermute | solution.py:232
  71.1 1.9 %copy-start.1 = (bf16[15,16,64,128]{3,2,1,0:T(8,128)(2,1)}, bf16[15,16,64,128]{3,2,1,0:T(8,128)(2,1)S(1)}, u32[]{:S(2)}) copy-start(bf16[15,16,64,128]{3,2,1,0:T(8,128)(2,1)S(1)} %unpack.2.wig_a_ref) | copy-start | bytes 11796484
  80.4 1.9 %copy-start.2 = (bf16[15,16,64,128]{3,2,1,0:T(8,128)(2,1)}, bf16[15,16,64,128]{3,2,1,0:T(8,128)(2,1)S(1)}, u32[]{:S(2)}) copy-start(bf16[15,16,64,128]{3,2,1,0:T(8,128)(2,1)S(1)} %unpack.3.wig_b_ref) | copy-start | bytes 11796484
Sparse Core Ops, SparseCore 0:
  8.9 32.3 all-gather.2

commit v3 on v2

--- a/solution.py
+++ b/solution.py
@@ -129,7 +129,7 @@
 
 
 def score_kernel(
-    tab_ref, rec_ref, lig_a_ref, lig_b_ref, wig_a_ref, wig_b_ref, out_ref, trans, rot, acc
+    where_ref, tab_ref, rec_ref, lig_a_ref, lig_b_ref, wig_a_ref, wig_b_ref, out_ref, trans, rot, acc
 ):
     step = pl.program_id(0)
     rots = wig_a_ref.shape[1]
@@ -180,7 +180,7 @@
                 ]
             return carry
 
-        lax.fori_loop(0, rots, one_rotation, 0, unroll=4)
+        lax.fori_loop(0, rots, one_rotation, 0, unroll=True)
 
     acc[...] += lax.dot_general(
         rot[...], trans[...], (((1,), (1,)), ((), ())), preferred_element_type=jnp.float32
@@ -228,10 +228,15 @@
     pieces = lig.reshape(nrec // 2, -1, 256)
     spread = lax.all_to_all(pieces, "rec", 0, 0, axis_index_groups=same_core)
     mine = lax.dynamic_index_in_dim(spread, lax.axis_index("rot"), 0, keepdims=False)
-    lig_a = lax.all_gather(mine, "rec", axis=0, axis_index_groups=same_core)
+    found = [mine]
+    for k in range(1, nrec // 2):
+        found.append(lax.ppermute(mine, "rec", [(i, i ^ (2 * k)) for i in range(nrec)]))
+    lig_a = jnp.concatenate(found, axis=0).reshape(padded, half * part, 256)
     lig_b = lax.ppermute(lig_a, "rec", swap)
-    lig_a = lig_a.reshape(padded, half * part, 256)
-    lig_b = lig_b.reshape(padded, half * part, 256)
+    each = padded // (nrec // 2)
+    order = jnp.arange(count, dtype=jnp.int32)
+    chip = (lax.axis_index("rec") // 2).astype(jnp.int32)
+    where = (chip ^ (order // each)) * each + order % each
 
     wig_a = unpack_wigner(turns_a, groups)
     wig_b = unpack_wigner(turns_b, groups)
@@ -252,25 +257,28 @@
 
     sums = pl.pallas_call(
         score_kernel,
-        grid=(count,),
-        in_specs=[
-            pl.BlockSpec((1, radial * dists, 2 * deep), lambda i: (i, 0, 0)),
-            pl.BlockSpec((1, 2 * deep, recs * 128), lambda i: (i, 0, 0)),
-            pl.BlockSpec((1, half * part, 256), lambda i: (i, 0, 0)),
-            pl.BlockSpec((1, half * part, 256), lambda i: (i, 0, 0)),
-            pl.BlockSpec((1, rots, SLOT, 128), lambda i: (i, 0, 0, 0)),
-            pl.BlockSpec((1, rots, SLOT, 128), lambda i: (i, 0, 0, 0)),
-        ],
-        out_specs=pl.BlockSpec((ligs, recs * dists), lambda i: (0, 0)),
+        grid_spec=pltpu.PrefetchScalarGridSpec(
+            num_scalar_prefetch=1,
+            grid=(count,),
+            in_specs=[
+                pl.BlockSpec((1, radial * dists, 2 * deep), lambda i, w: (i, 0, 0)),
+                pl.BlockSpec((1, 2 * deep, recs * 128), lambda i, w: (i, 0, 0)),
+                pl.BlockSpec((1, half * part, 256), lambda i, w: (w[i], 0, 0)),
+                pl.BlockSpec((1, half * part, 256), lambda i, w: (w[i], 0, 0)),
+                pl.BlockSpec((1, rots, SLOT, 128), lambda i, w: (i, 0, 0, 0)),
+                pl.BlockSpec((1, rots, SLOT, 128), lambda i, w: (i, 0, 0, 0)),
+            ],
+            out_specs=pl.BlockSpec((ligs, recs * dists), lambda i, w: (0, 0)),
+            scratch_shapes=[
+                pltpu.VMEM((recs * dists, half * 256), jnp.bfloat16),
+                pltpu.VMEM((2 * rots * ligs, half * 256), jnp.bfloat16),
+                pltpu.VMEM((2 * rots * ligs, recs * dists), jnp.float32),
+            ],
+        ),
         out_shape=jax.ShapeDtypeStruct((ligs, recs * dists), jnp.float32),
-        scratch_shapes=[
-            pltpu.VMEM((recs * dists, half * 256), jnp.bfloat16),
-            pltpu.VMEM((2 * rots * ligs, half * 256), jnp.bfloat16),
-            pltpu.VMEM((2 * rots * ligs, recs * dists), jnp.float32),
-        ],
         compiler_params=params,
         name="scores",
-    )(tab, rec, lig_a, lig_b, wig_a, wig_b)
+    )(where, tab, rec, lig_a, lig_b, wig_a, wig_b)
     totals = jnp.sum(sums.reshape(2, part, recs, dists), axis=3)
     totals = jnp.where(core == 0, totals, totals[::-1]).reshape(ligs, recs)
     return jnp.log(totals.T)

time: 158 us -> 114 us (0.72)
  Pallas kernels: 85.3 us -> 55.7 us
  blocking collectives: 15.2 us -> 0 us
  waiting for transfers between devices: 1.28 us -> 5.87 us
  starting transfers between devices: 5.24 us -> 9.07 us
  local copies, waits for them, and re-layouts: 27.3 us -> 23.6 us
  other arithmetic: 8.57 us -> 5.85 us
    pallas_call x1, Pallas kernels: 66.6 us -> 37 us  [per_device(): pl.pallas_call(score_kernel, grid_spec=pltpu.PrefetchScalarGridSpec(num_s...]
    all_gather x1 -> x0, blocking collectives: 15.2 us -> none  [per_device(): lig_a = lax.all_gather(mine, 'rec', axis=0, axis_index_groups=same_core)]
    all_to_all x1, waiting for transfers between devices: 0.01 us -> 5.82 us  [per_device(): spread = lax.all_to_all(pieces, 'rec', 0, 0, axis_index_groups=same_core)]
    unnamed x14, other arithmetic: 8.35 us -> 4.05 us
    ppermute x0 -> x3, starting transfers between devices: none -> 3.49 us  [per_device(): lax.ppermute(mine, 'rec', [(i, i ^ 2 * k) for i in range(nrec)])]
    squeeze x0 -> x1, local copies, waits for them, and re-layouts: none -> 1.68 us  [per_device(): lax.dynamic_index_in_dim(spread, lax.axis_index('rot'), 0, keepdims=False)]
    dynamic_slice x1 -> x0, local copies, waits for them, and re-layouts: 1.66 us -> none  [per_device(): lax.dynamic_index_in_dim(spread, lax.axis_index('rot'), 0, keepdims=False)]
    unnamed x37 -> x41, local copies, waits for them, and re-layouts: 10.8 us -> 10.8 us
  transfers between devices with their start and end apart: 4 -> 7, of which waited for: 1 -> 1; matrix products, arithmetic and copies ran while one was open for 17% -> 20% of each run, Pallas kernels for 12% -> 16%
where the time goes in v3:
time: 114 us
  Pallas kernels  55.7 us (49%)
  local copies, waits for them, and re-layouts  23.6 us (21%)
  between operations  13.8 us (12%)
  starting transfers between devices  9.07 us (8%)
  waiting for transfers between devices  5.87 us (5%)
  other arithmetic  5.85 us (5%)
    pallas_call x1, Pallas kernels, per_device(): pl.pallas_call(score_kernel, grid_spec=pltpu.PrefetchScalarGridSpec(num_s...  37 us
    pallas_call x2, Pallas kernels, unpack_wigner(): pl.pallas_call(functools.partial(unpack_kernel, groups, front), grid=(row...  14.8 us
    unnamed x41, local copies, waits for them, and re-layouts  10.8 us
    all_to_all x1, waiting for transfers between devices, per_device(): spread = lax.all_to_all(pieces, 'rec', 0, 0, axis_index_groups=same_core)  5.82 us
    gather x1, local copies, waits for them, and re-layouts, per_device(): tables = jnp.transpose(trans_table[dist_index], (1, 2, 0, 3))  5.48 us
    all_to_all x1, starting transfers between devices, per_device(): spread = lax.all_to_all(pieces, 'rec', 0, 0, axis_index_groups=same_core)  5.16 us
    unnamed x14, other arithmetic  4.05 us
    ppermute x3, starting transfers between devices, per_device(): lax.ppermute(mine, 'rec', [(i, i ^ 2 * k) for i in range(nrec)])  3.49 us
  transfers between devices with their start and end apart: 7, of which 1 were waited for; matrix products, arithmetic and copies ran while one was open for 20% of the time, Pallas kernels for 16%

profile of v3, /device:TPU:0, one launch (start us, length us, event | category | flops | bytes accessed | tf_op | source)
XLA Modules:
  0.0 113.9 jit_solution(11356661280485946769)
XLA Ops:
  6.5 0.0 copy-start
  6.5 0.0 all-gather.3.cloned.1.call-start
  6.5 1.1 copy-done
  7.6 0.9 dynamic-slice_bitcast_fusion
  8.5 0.0 all-gather.3.cloned.1.call-update
  8.5 1.3 %copy.11 = bf16[8,2,2,15,900]{4,0,3,1,2:T(8,128)(2,1)S(1)} copy(bf16[8,2,2,15,900]{4,0,3,2,1:T(8,128)(2,1)} %bitcast.81) | data formatting | bytes 1728000 | tf_op jit(solution)/shard_map/reshape | solution.py:220
  9.8 0.0 copy-done.3
  9.8 0.0 copy-start.18
  9.8 2.3 %ligand_slots.1 = bf16[16,120,256]{2,1,0:T(8,128)(2,1)} custom-call(s32[1,1024]{1,0:T(1,128)S(1)} %copy-done.3, bf16[480,900]{1,0:T(8,128)(2,1)S(1)} %bitcast.76), custom_call_target="tpu_custom_call" | custom-call | tf_op jit(solution)/shard_map/ligand_slots/pallas_call | solution.py:222
  12.1 5.2 %all-to-all-start = ((bf16[4,480,256]{2,1,0:T(8,128)(2,1)}), bf16[4,480,256]{2,1,0:T(8,128)(2,1)}, u32[]{:S(2)}, u32[]{:S(2)}) async-start(bf16[4,480,256]{2,1,0:T(8,128)(2,1)} %bitcast.35), calls=%async_computation | async-start | bytes 1966080 | tf_op jit(solution)/shard_map/all_to_all | solution.py:229
  17.3 0.0 copy-done.18
  17.3 5.5 %gather_fusion = bf16[8,30,30,30]{3,0,2,1:T(8,128)(2,1)S(1)} fusion(bf16[16,30,30,30]{3,0,2,1:T(8,128)(2,1)} %param.9, s32[1024]{0:T(1024)S(1)} %pad_clamp_fusion), kind=kCustom, calls=%fused_computation | custom fusion | bytes 864032 | tf_op jit(solution)/shard_map/gather | solution.py:253
  22.8 0.8 slice_bitcast_fusion.19
  23.5 0.1 maximum_dynamic-update-slice_fusion.14
  23.6 0.1 maximum_dynamic-update-slice_fusion.13
  23.7 0.1 maximum_dynamic-update-slice_fusion.12
  23.8 0.1 maximum_dynamic-update-slice_fusion.11
  23.9 1.1 slice_bitcast_fusion.1
  25.1 5.8 %all-to-all-done = bf16[4,480,256]{2,1,0:T(8,128)(2,1)} async-done(((bf16[4,480,256]{2,1,0:T(8,128)(2,1)}), bf16[4,480,256]{2,1,0:T(8,128)(2,1)}, u32[]{:S(2)}, u32[]{:S(2)}) %all-to-all-start) | async-done | bytes 983072 | tf_op jit(solution)/shard_map/all_to_all | solution.py:229
  30.9 1.7 %dynamic-slice_bitcast_fusion.1 = bf16[480,256]{1,0:T(8,128)(2,1)} fusion(bf16[4,480,256]{2,1,0:T(8,128)(2,1)} %all-to-all-done, s32[]{:T(128)S(6)} %select_n.46), kind=kLoop, calls=%fused_computation.3 | loop fusion | bytes 491524 | tf_op jit(solution)/shard_map/jit(dynamic_index_in_dim)/squeeze | solution.py:230
  32.5 1.5 %collective-permute-start = (bf16[480,256]{1,0:T(8,128)(2,1)}, bf16[480,256]{1,0:T(8,128)(2,1)}, u32[]{:S(2)}, u32[]{:S(2)}) collective-permute-start(bf16[480,256]{1,0:T(8,128)(2,1)} %dynamic-slice_bitcast_fusion.1), channel_id=1, source_target_pairs={{0,8},{4,12},{8,0},{12,4},{16,24},{20,28},{24,16},{28,20},{1,9},{5... | collective-permute-start | bytes 737288 | tf_op jit(solution)/shard_map/ppermute | solution.py:233
  34.0 0.5 collective-permute-start.1
  34.5 1.5 %collective-permute-start.2 = (bf16[480,256]{1,0:T(8,128)(2,1)}, bf16[480,256]{1,0:T(8,128)(2,1)}, u32[]{:S(2)}, u32[]{:S(2)}) collective-permute-start(bf16[480,256]{1,0:T(8,128)(2,1)} %dynamic-slice_bitcast_fusion.1), channel_id=1, source_target_pairs={{0,24},{4,28},{8,16},{12,20},{16,8},{20,12},{24,0},{28,4},{1,25},{... | collective-permute-start | bytes 737288 | tf_op jit(solution)/shard_map/ppermute | solution.py:233
  36.0 0.1 maximum_dynamic-update-slice_fusion.10
  36.2 2.7 %copy.10 = bf16[8,60,900]{2,1,0:T(8,128)(2,1)} copy(bf16[8,60,900]{2,0,1:T(8,128)(2,1)} %param.6) | data formatting | bytes 1728000 | tf_op args[0]
  38.9 1.5 %reshape.114 = bf16[16,30,900]{2,1,0:T(8,128)(2,1)S(1)} reshape(bf16[8,60,900]{2,1,0:T(8,128)(2,1)} %copy.10) | data formatting | bytes 1728000 | tf_op jit(solution)/shard_map/reshape | solution.py:245
  40.3 0.2 pad.16
  40.5 1.6 %receptor_slots.1.rec_ref = bf16[15,64,1024]{2,1,0:T(8,128)(2,1)S(1)} custom-call(s32[1,1024]{1,0:T(1,128)S(1)} %copy-done.3, bf16[512,900]{1,0:T(8,128)(2,1)S(1)} %bitcast.75), custom_call_target="tpu_custom_call" | custom-call | tf_op jit(solution)/shard_map/receptor_slots/pallas_call | solution.py:247
  42.1 1.0 maximum_dynamic-update-slice_fusion.9
  43.1 1.0 maximum_dynamic-update-slice_fusion.8
  44.0 0.0 all-gather.3.cloned.1.call-done
  44.1 2.4 %reshape.131 = bf16[16,35990]{1,0:T(8,128)(2,1)} reshape(bf16[4,4,35990]{2,1,0:T(4,128)(2,1)} %all-gather.3.cloned.1.call-done) | data formatting | bytes 2303360
  46.4 0.0 copy-start.15
  46.4 0.0 copy-start.12
  46.5 0.1 collective-permute-start.4
  46.6 0.0 collective-permute-done
  46.6 0.0 collective-permute-done.1
  46.6 0.0 collective-permute-done.2
  46.7 1.6 %pad_maximum_fusion = bf16[1920,256]{1,0:T(8,128)(2,1)S(1)} fusion(bf16[480,256]{1,0:T(8,128)(2,1)} %collective-permute-done.2, bf16[480,256]{1,0:T(8,128)(2,1)} %collective-permute-done.1, bf16[480,256]{1,0:T(8,128)(2,1)} %collective-permute-done, bf16[480,256]{1,0:T(8,128)(2,1)} %dynamic-slice_bitcast_fusion.1), kind=kLoop, calls=%fused_computation.1 | loop fusion | flops 3932160 | bytes 1966080 | tf_op jit(solution)/shard_map/concatenate | solution.py:234
  48.2 0.3 collective-permute-start.3
  48.6 1.0 maximum_dynamic-update-slice_fusion.7
  49.6 0.1 maximum_dynamic-update-slice_fusion.6
  49.7 0.0 copy-done.15
  49.7 0.1 maximum_dynamic-update-slice_fusion.5
  49.8 0.1 maximum_dynamic-update-slice_fusion.4
  49.9 0.0 copy-done.11
  49.9 0.1 maximum_dynamic-update-slice_fusion.3
  50.1 0.0 copy-done.9
  50.1 0.1 maximum_dynamic-update-slice_fusion.2
  50.2 0.1 maximum_dynamic-update-slice_fusion.1
  50.3 0.1 maximum_dynamic-update-slice_fusion.tab_ref
  50.4 0.1 pad.17.w_ref
  50.5 7.4 %unpack.2.wig_a_ref = bf16[15,16,64,128]{3,2,1,0:T(8,128)(2,1)S(1)} custom-call(bf16[16,36480]{1,0:T(8,128)(2,1)S(1)} %pad.17.w_ref), custom_call_target="tpu_custom_call" | custom-call | tf_op jit(solution)/shard_map/unpack/pallas_call | solution.py:119
  57.9 0.0 copy-start.1
  57.9 1.9 %copy-done.1 = bf16[15,16,64,128]{3,2,1,0:T(8,128)(2,1)} copy-done((bf16[15,16,64,128]{3,2,1,0:T(8,128)(2,1)}, bf16[15,16,64,128]{3,2,1,0:T(8,128)(2,1)S(1)}, u32[]{:S(2)}) %copy-start.1) | copy-done | bytes 3932184
  59.8 0.0 collective-permute-done.4
  59.8 0.1 pad.18.w_ref
  59.9 7.4 %unpack.3.wig_b_ref = bf16[15,16,64,128]{3,2,1,0:T(8,128)(2,1)S(1)} custom-call(bf16[16,36480]{1,0:T(8,128)(2,1)S(1)} %pad.18.w_ref), custom_call_target="tpu_custom_call" | custom-call | tf_op jit(solution)/shard_map/unpack/pallas_call | solution.py:119
  67.3 1.9 %copy-done.2 = bf16[15,16,64,128]{3,2,1,0:T(8,128)(2,1)} copy-done((bf16[15,16,64,128]{3,2,1,0:T(8,128)(2,1)}, bf16[15,16,64,128]{3,2,1,0:T(8,128)(2,1)S(1)}, u32[]{:S(2)}) %copy-start.2) | copy-done | bytes 3932184
  69.2 0.0 collective-permute-done.3.lig_b_ref
  69.2 37.0 %scores.1 = f32[16,64]{1,0:T(8,128)S(1)} custom-call(s32[15]{0:T(128)S(1)} %fusion.2.where_ref, bf16[15,240,64]{2,1,0:T(8,128)(2,1)S(1)} %maximum_dynamic-update-slice_fusion.tab_ref, bf16[15,64,1024]{2,1,0:T(8,128)(2,1)S(1)} %receptor_slots.1.rec_ref, bf16[16,120,256]{2,1,0:T(8,128)(2,1)S(1)} %bitcast.78, ...), custom_call_target="tpu_custom_call" | custom-call | tf_op jit(solution)/shard_map/scores/pallas_call | solution.py:258
  106.2 0.1 reshape.120
  106.3 0.1 reduce_sum.9
  106.4 0.7 copy.13
  (29 shorter events, 0.1 us)
Async XLA Ops:
  6.5 1.1 copy-start
  6.5 3.2 %copy-start.3 = (s32[1,1024]{1,0:T(1,128)S(1)}, s32[1,1024]{1,0:T(1,128)}, u32[]{:S(2)}) copy-start(s32[1,1024]{1,0:T(1,128)} %constant.86.source_ref) | copy-start | bytes 12292
  6.5 37.5 %all-gather.3.cloned.1.call-start = ((), (), s32[]{:S(2)}) async-start(), calls=%async_computation.1 | async-start | bytes 1443840 | tf_op jit(solution)/shard_map/all_gather | solution.py:216
  9.8 7.5 %copy-start.18 = (s32[8]{0:T(128)S(1)}, s32[8]{0:T(128)}, u32[]{:S(2)}) copy-start(s32[8]{0:T(128)} %param.10) | copy-start | bytes 100
  12.1 18.8 %all-to-all-start = ((bf16[4,480,256]{2,1,0:T(8,128)(2,1)}), bf16[4,480,256]{2,1,0:T(8,128)(2,1)}, u32[]{:S(2)}, u32[]{:S(2)}) async-start(bf16[4,480,256]{2,1,0:T(8,128)(2,1)} %bitcast.35), calls=%async_computation | async-start | bytes 1966080 | tf_op jit(solution)/shard_map/all_to_all | solution.py:229
  32.5 14.1 %collective-permute-start = (bf16[480,256]{1,0:T(8,128)(2,1)}, bf16[480,256]{1,0:T(8,128)(2,1)}, u32[]{:S(2)}, u32[]{:S(2)}) collective-permute-start(bf16[480,256]{1,0:T(8,128)(2,1)} %dynamic-slice_bitcast_fusion.1), channel_id=1, source_target_pairs={{0,8},{4,12},{8,0},{12,4},{16,24},{20,28},{24,16},{28,20},{1,9},{5... | collective-permute-start | bytes 737288 | tf_op jit(solution)/shard_map/ppermute | solution.py:233
  34.0 12.6 %collective-permute-start.1 = (bf16[480,256]{1,0:T(8,128)(2,1)}, bf16[480,256]{1,0:T(8,128)(2,1)}, u32[]{:S(2)}, u32[]{:S(2)}) collective-permute-start(bf16[480,256]{1,0:T(8,128)(2,1)} %dynamic-slice_bitcast_fusion.1), channel_id=1, source_target_pairs={{0,16},{4,20},{8,24},{12,28},{16,0},{20,4},{24,8},{28,12},{1,17},{... | collective-permute-start | bytes 737288 | tf_op jit(solution)/shard_map/ppermute | solution.py:233
  34.5 12.1 %collective-permute-start.2 = (bf16[480,256]{1,0:T(8,128)(2,1)}, bf16[480,256]{1,0:T(8,128)(2,1)}, u32[]{:S(2)}, u32[]{:S(2)}) collective-permute-start(bf16[480,256]{1,0:T(8,128)(2,1)} %dynamic-slice_bitcast_fusion.1), channel_id=1, source_target_pairs={{0,24},{4,28},{8,16},{12,20},{16,8},{20,12},{24,0},{28,4},{1,25},{... | collective-permute-start | bytes 737288 | tf_op jit(solution)/shard_map/ppermute | solution.py:233
  46.4 3.1 %copy-start.16 = (bf16[1,240,32]{2,1,0:T(8,128)(2,1)S(1)}, bf16[1,240,32]{2,1,0:T(8,128)(2,1)}, u32[]{:S(2)}) copy-start(bf16[1,240,32]{2,1,0:T(8,128)(2,1)} %get-tuple-element.17) | copy-start | bytes 46084
  46.4 3.1 %copy-start.17 = (bf16[1,240,32]{2,1,0:T(8,128)(2,1)S(1)}, bf16[1,240,32]{2,1,0:T(8,128)(2,1)}, u32[]{:S(2)}) copy-start(bf16[1,240,32]{2,1,0:T(8,128)(2,1)} %get-tuple-element.18) | copy-start | bytes 46084
  46.4 3.2 %copy-start.14 = (bf16[1,240,32]{2,1,0:T(8,128)(2,1)S(1)}, bf16[1,240,32]{2,1,0:T(8,128)(2,1)}, u32[]{:S(2)}) copy-start(bf16[1,240,32]{2,1,0:T(8,128)(2,1)} %get-tuple-element.15) | copy-start | bytes 46084
  46.4 3.3 %copy-start.15 = (bf16[1,240,32]{2,1,0:T(8,128)(2,1)S(1)}, bf16[1,240,32]{2,1,0:T(8,128)(2,1)}, u32[]{:S(2)}) copy-start(bf16[1,240,32]{2,1,0:T(8,128)(2,1)} %get-tuple-element.16) | copy-start | bytes 46084
  46.4 3.4 %copy-start.12 = (bf16[1,240,32]{2,1,0:T(8,128)(2,1)S(1)}, bf16[1,240,32]{2,1,0:T(8,128)(2,1)}, u32[]{:S(2)}) copy-start(bf16[1,240,32]{2,1,0:T(8,128)(2,1)} %get-tuple-element.13) | copy-start | bytes 46084
  46.5 3.4 %copy-start.13 = (bf16[1,240,32]{2,1,0:T(8,128)(2,1)S(1)}, bf16[1,240,32]{2,1,0:T(8,128)(2,1)}, u32[]{:S(2)}) copy-start(bf16[1,240,32]{2,1,0:T(8,128)(2,1)} %get-tuple-element.14) | copy-start | bytes 46084
  46.5 3.5 %copy-start.10 = (bf16[1,240,32]{2,1,0:T(8,128)(2,1)S(1)}, bf16[1,240,32]{2,1,0:T(8,128)(2,1)}, u32[]{:S(2)}) copy-start(bf16[1,240,32]{2,1,0:T(8,128)(2,1)} %get-tuple-element.11) | copy-start | bytes 46084
  46.5 3.5 %copy-start.11 = (bf16[1,240,32]{2,1,0:T(8,128)(2,1)S(1)}, bf16[1,240,32]{2,1,0:T(8,128)(2,1)}, u32[]{:S(2)}) copy-start(bf16[1,240,32]{2,1,0:T(8,128)(2,1)} %get-tuple-element.12) | copy-start | bytes 46084
  46.5 3.6 %copy-start.8 = (bf16[1,240,32]{2,1,0:T(8,128)(2,1)S(1)}, bf16[1,240,32]{2,1,0:T(8,128)(2,1)}, u32[]{:S(2)}) copy-start(bf16[1,240,32]{2,1,0:T(8,128)(2,1)} %get-tuple-element.9) | copy-start | bytes 46084
  46.5 3.6 %copy-start.9 = (bf16[1,240,32]{2,1,0:T(8,128)(2,1)S(1)}, bf16[1,240,32]{2,1,0:T(8,128)(2,1)}, u32[]{:S(2)}) copy-start(bf16[1,240,32]{2,1,0:T(8,128)(2,1)} %get-tuple-element.10) | copy-start | bytes 46084
  46.5 3.7 %copy-start.6 = (bf16[1,240,32]{2,1,0:T(8,128)(2,1)S(1)}, bf16[1,240,32]{2,1,0:T(8,128)(2,1)}, u32[]{:S(2)}) copy-start(bf16[1,240,32]{2,1,0:T(8,128)(2,1)} %get-tuple-element.7) | copy-start | bytes 46084
  46.5 3.7 %copy-start.7 = (bf16[1,240,32]{2,1,0:T(8,128)(2,1)S(1)}, bf16[1,240,32]{2,1,0:T(8,128)(2,1)}, u32[]{:S(2)}) copy-start(bf16[1,240,32]{2,1,0:T(8,128)(2,1)} %get-tuple-element.8) | copy-start | bytes 46084
  46.5 3.8 %copy-start.5 = (bf16[1,240,32]{2,1,0:T(8,128)(2,1)S(1)}, bf16[1,240,32]{2,1,0:T(8,128)(2,1)}, u32[]{:S(2)}) copy-start(bf16[1,240,32]{2,1,0:T(8,128)(2,1)} %get-tuple-element.6) | copy-start | bytes 46084
  46.5 3.9 %copy-start.4 = (bf16[16,35990]{1,0:T(8,128)(2,1)S(1)}, bf16[16,35990]{1,0:T(8,128)(2,1)}, u32[]{:S(2)}) copy-start(bf16[16,35990]{1,0:T(8,128)(2,1)} %reshape.131) | copy-start | bytes 3455044
  46.5 13.3 %collective-permute-start.4 = (bf16[16,35990]{1,0:T(8,128)(2,1)}, bf16[16,35990]{1,0:T(8,128)(2,1)S(1)}, u32[]{:S(2)}, u32[]{:S(2)}) collective-permute-start(bf16[16,35990]{1,0:T(8,128)(2,1)} %reshape.131), channel_id=1, source_target_pairs={{0,4},{4,0},{8,12},{12,8},{16,20},{20,16},{24,28},{28,24},{1,5},{5... | collective-permute-start | bytes 3455048 | tf_op jit(solution)/shard_map/ppermute | solution.py:217
  48.2 21.0 %collective-permute-start.3 = (bf16[16,120,256]{2,1,0:T(8,128)(2,1)S(1)}, bf16[16,120,256]{2,1,0:T(8,128)(2,1)S(1)}, u32[]{:S(2)}, u32[]{:S(2)}) collective-permute-start(bf16[16,120,256]{2,1,0:T(8,128)(2,1)S(1)} %bitcast.77), channel_id=1, source_target_pairs={{0,4},{4,0},{8,12},{12,8},{16,20},{20,16},{24,28},{28,24},{1,5},{5... | collective-permute-start | bytes 2949128 | tf_op jit(solution)/shard_map/ppermute | solution.py:235
  57.9 1.9 %copy-start.1 = (bf16[15,16,64,128]{3,2,1,0:T(8,128)(2,1)}, bf16[15,16,64,128]{3,2,1,0:T(8,128)(2,1)S(1)}, u32[]{:S(2)}) copy-start(bf16[15,16,64,128]{3,2,1,0:T(8,128)(2,1)S(1)} %unpack.2.wig_a_ref) | copy-start | bytes 11796484
  67.3 1.9 %copy-start.2 = (bf16[15,16,64,128]{3,2,1,0:T(8,128)(2,1)}, bf16[15,16,64,128]{3,2,1,0:T(8,128)(2,1)S(1)}, u32[]{:S(2)}) copy-start(bf16[15,16,64,128]{3,2,1,0:T(8,128)(2,1)S(1)} %unpack.3.wig_b_ref) | copy-start | bytes 11796484
Sparse Core Ops, SparseCore 0:
  8.9 32.3 all-gather.2

commit v4 on v3

--- a/solution.py
+++ b/solution.py
@@ -88,8 +88,11 @@
             out_ref[group, :, r * 128 : (r + 1) * 128] = both.astype(jnp.bfloat16)
 
 
-def unpack_kernel(groups, front, w_ref, out_ref, scr):
-    rows = w_ref.shape[0]
+def unpack_kernel(groups, w_ref, out_ref, flat, scr):
+    blocks, share, width = w_ref.shape
+    rows = blocks * share
+    for part in range(blocks):
+        flat[part * share : (part + 1) * share, :width] = w_ref[part].astype(jnp.float32)
     lane = lax.broadcasted_iota(jnp.int32, (rows, 128), 1)
     for index, members in enumerate(groups):
         used = 0
@@ -97,13 +100,19 @@
             extent = 2 * d + 1
             keep = (lane >= used) & (lane < used + extent)
             for m in range(extent):
-                start = front + packed_start(d) + m * extent - used
+                start = packed_start(d) + m * extent
                 base = start // 128 * 128
-                window = w_ref[:, base : base + 256].astype(jnp.float32)
-                shift = start - base
+                shift = (used - start) % 128
+                window = flat[:, base : base + 128]
                 if shift:
-                    window = pltpu.roll(window, 256 - shift, 1)
-                scr[:, used + m, :] = jnp.where(keep, window[:, :128], 0.0)
+                    window = pltpu.roll(window, shift, 1)
+                first = base + 128 - start
+                if first < extent:
+                    rest = flat[:, base + 128 : base + 256]
+                    if shift:
+                        rest = pltpu.roll(rest, shift, 1)
+                    window = jnp.where(lane < used + first, window, rest)
+                scr[:, used + m, :] = jnp.where(keep, window, 0.0)
             used += extent
         for m in range(used, SLOT):
             scr[:, m, :] = jnp.zeros((rows, 128), jnp.float32)
@@ -111,39 +120,61 @@
 
 
 def unpack_wigner(wigner, groups):
-    front = 128
-    rows, width = wigner.shape
-    total = (front + width + 127) // 128 * 128 + 256
-    padded = jnp.pad(wigner, ((0, 0), (front, total - front - width)))
-    qstep = 8 if rows % 16 else 16
+    parts, share, width = wigner.shape
+    rows = parts * share
+    blocks = math.gcd(parts, max(16 // share, 1))
+    qstep = blocks * share
+    total = (width + 127) // 128 * 128 + 128
     return pl.pallas_call(
-        functools.partial(unpack_kernel, groups, front),
-        grid=(rows // qstep,),
-        in_specs=[pl.BlockSpec((qstep, total), lambda i: (i, 0))],
+        functools.partial(unpack_kernel, groups),
+        grid=(parts // blocks,),
+        in_specs=[pl.BlockSpec((blocks, share, width), lambda i: (i, 0, 0))],
         out_specs=pl.BlockSpec((len(groups), qstep, SLOT, 128), lambda i: (0, i, 0, 0)),
         out_shape=jax.ShapeDtypeStruct((len(groups), rows, SLOT, 128), jnp.bfloat16),
-        scratch_shapes=[pltpu.VMEM((qstep, SLOT, 128), jnp.float32)],
+        scratch_shapes=[
+            pltpu.VMEM((qstep, total), jnp.float32),
+            pltpu.VMEM((qstep, SLOT, 128), jnp.float32),
+        ],
         compiler_params=pltpu.CompilerParams(vmem_limit_bytes=48 * 1024 * 1024),
         name="unpack",
-    )(padded)
+    )(wigner)
 
 
 def score_kernel(
-    where_ref, tab_ref, rec_ref, lig_a_ref, lig_b_ref, wig_a_ref, wig_b_ref, out_ref, trans, rot, acc
+    where_ref,
+    one_ref,
+    two_ref,
+    tab_a_ref,
+    tab_b_ref,
+    rec_ref,
+    lig_a_ref,
+    lig_b_ref,
+    wig_a_ref,
+    wig_b_ref,
+    out_ref,
+    table,
+    trans,
+    rot,
+    acc,
 ):
     step = pl.program_id(0)
     rots = wig_a_ref.shape[1]
     recs = rec_ref.shape[2] // 128
     rad = trans.shape[1] // 256
-    dists = tab_ref.shape[1] // (2 * rad)
+    dists = tab_a_ref.shape[1] // (2 * rad)
+    radial = tab_a_ref.shape[2]
     part = lig_a_ref.shape[1] // rad
     ligs = 2 * part
 
     @pl.when(step == 0)
     def _():
         acc[...] = jnp.zeros_like(acc)
-
-    moved = jnp.dot(tab_ref[0], rec_ref[0], preferred_element_type=jnp.float32)
+        table[...] = jnp.zeros_like(table)
+
+    deep = table.shape[1] // 2
+    table[:, :radial] = tab_a_ref[0]
+    table[:, deep : deep + radial] = tab_b_ref[0]
+    moved = jnp.dot(table[...], rec_ref[0], preferred_element_type=jnp.float32)
     moved = moved.reshape(2, rad, dists, recs * 128)
     for xq in range(rad):
         for half in range(2):
@@ -213,9 +244,9 @@
 
     share = wigner.shape[0] // 2
     own = lax.dynamic_slice_in_dim(wigner, core * share, share, 0)
-    turns_a = lax.all_gather(own, "rot", axis=0, tiled=True)
+    turns_a = lax.all_gather(own, "rot", axis=0)
     turns_b = lax.ppermute(turns_a, "rec", swap)
-    rots = turns_a.shape[0]
+    rots = turns_a.shape[0] * share
 
     lig = ligands.reshape(part, props, 2, half, angular)
     lig = jnp.transpose(lig, (2, 1, 3, 0, 4)).reshape(4 * half * part, angular)
@@ -251,25 +282,27 @@
         name="receptor_slots",
     )(source, rec)
     tables = jnp.transpose(trans_table[dist_index], (1, 2, 0, 3))
-    tables = jnp.pad(tables, ((0, 0), (0, 0), (0, 0), (0, deep - radial)))
-    tab = jnp.stack([jnp.concatenate([tables[d] for d in row], axis=-1) for row in groups])
-    tab = tab.reshape(count, radial * dists, 2 * deep)
+    tables = tables.reshape(degrees, radial * dists, radial)
+    one = jnp.array([members[0] for members in groups], jnp.int32)
+    two = jnp.array([members[-1] for members in groups], jnp.int32)
 
     sums = pl.pallas_call(
         score_kernel,
         grid_spec=pltpu.PrefetchScalarGridSpec(
-            num_scalar_prefetch=1,
+            num_scalar_prefetch=3,
             grid=(count,),
             in_specs=[
-                pl.BlockSpec((1, radial * dists, 2 * deep), lambda i, w: (i, 0, 0)),
-                pl.BlockSpec((1, 2 * deep, recs * 128), lambda i, w: (i, 0, 0)),
-                pl.BlockSpec((1, half * part, 256), lambda i, w: (w[i], 0, 0)),
-                pl.BlockSpec((1, half * part, 256), lambda i, w: (w[i], 0, 0)),
-                pl.BlockSpec((1, rots, SLOT, 128), lambda i, w: (i, 0, 0, 0)),
-                pl.BlockSpec((1, rots, SLOT, 128), lambda i, w: (i, 0, 0, 0)),
+                pl.BlockSpec((1, radial * dists, radial), lambda i, w, one, two: (one[i], 0, 0)),
+                pl.BlockSpec((1, radial * dists, radial), lambda i, w, one, two: (two[i], 0, 0)),
+                pl.BlockSpec((1, 2 * deep, recs * 128), lambda i, w, one, two: (i, 0, 0)),
+                pl.BlockSpec((1, half * part, 256), lambda i, w, one, two: (w[i], 0, 0)),
+                pl.BlockSpec((1, half * part, 256), lambda i, w, one, two: (w[i], 0, 0)),
+                pl.BlockSpec((1, rots, SLOT, 128), lambda i, w, one, two: (i, 0, 0, 0)),
+                pl.BlockSpec((1, rots, SLOT, 128), lambda i, w, one, two: (i, 0, 0, 0)),
             ],
-            out_specs=pl.BlockSpec((ligs, recs * dists), lambda i, w: (0, 0)),
+            out_specs=pl.BlockSpec((ligs, recs * dists), lambda i, w, one, two: (0, 0)),
             scratch_shapes=[
+                pltpu.VMEM((radial * dists, 2 * deep), jnp.bfloat16),
                 pltpu.VMEM((recs * dists, half * 256), jnp.bfloat16),
                 pltpu.VMEM((2 * rots * ligs, half * 256), jnp.bfloat16),
                 pltpu.VMEM((2 * rots * ligs, recs * dists), jnp.float32),
@@ -278,7 +311,7 @@
         out_shape=jax.ShapeDtypeStruct((ligs, recs * dists), jnp.float32),
         compiler_params=params,
         name="scores",
-    )(where, tab, rec, lig_a, lig_b, wig_a, wig_b)
+    )(where, one, two, tables, tables, rec, lig_a, lig_b, wig_a, wig_b)
     totals = jnp.sum(sums.reshape(2, part, recs, dists), axis=3)
     totals = jnp.where(core == 0, totals, totals[::-1]).reshape(ligs, recs)
     return jnp.log(totals.T)

time: 114 us -> 123 us (1.079)
  waiting for transfers between devices: 5.87 us -> 22.5 us
  other arithmetic: 5.85 us -> 0.18 us
  local copies, waits for them, and re-layouts: 23.6 us -> 19 us
  Pallas kernels: 55.7 us -> 58.2 us
    all_gather x1, waiting for transfers between devices: 0.02 us -> 7.44 us  [per_device(): turns_a = lax.all_gather(own, 'rot', axis=0)]
    all_to_all x1, waiting for transfers between devices: 5.82 us -> 12.9 us  [per_device(): spread = lax.all_to_all(pieces, 'rec', 0, 0, axis_index_groups=same_core)]
    unnamed x14 -> x0, other arithmetic: 4.05 us -> none
    ppermute x3, waiting for transfers between devices: 0.01 us -> 2.08 us  [per_device(): lax.ppermute(mine, 'rec', [(i, i ^ 2 * k) for i in range(nrec)])]
    concatenate x2 -> x0, local copies, waits for them, and re-layouts: 1.85 us -> none  [per_device(): jnp.concatenate([tables[d] for d in row], axis=-1)]
    squeeze x1, local copies, waits for them, and re-layouts: 1.68 us -> 0.02 us  [per_device(): lax.dynamic_index_in_dim(spread, lax.axis_index('rot'), 0, keepdims=False)]
    concatenate x1, other arithmetic: 1.57 us -> 0.06 us  [per_device(): lig_a = jnp.concatenate(found, axis=0).reshape(padded, half * part, 256)]
    pallas_call x2, Pallas kernels: 14.8 us -> 16.1 us  [unpack_wigner(): pl.pallas_call(functools.partial(unpack_kernel, groups), grid=(parts // b...]
  transfers between devices with their start and end apart: 7 -> 7, of which waited for: 1 -> 3; matrix products, arithmetic and copies ran while one was open for 20% -> 8% of each run, Pallas kernels for 16% -> 16%
where the time goes in v4:
time: 123 us; the launch traced here: 122 us
  Pallas kernels  58.2 us (47%)
  waiting for transfers between devices  22.5 us (18%)
  local copies, waits for them, and re-layouts  19 us (15%)
  between operations  13.6 us (11%)
  starting transfers between devices  8.92 us (7%)
    pallas_call x1, Pallas kernels, per_device(): pl.pallas_call(score_kernel, grid_spec=pltpu.PrefetchScalarGridSpec(num_s...  38.1 us
    pallas_call x2, Pallas kernels, unpack_wigner(): pl.pallas_call(functools.partial(unpack_kernel, groups), grid=(parts // b...  16.1 us
    all_to_all x1, waiting for transfers between devices, per_device(): spread = lax.all_to_all(pieces, 'rec', 0, 0, axis_index_groups=same_core)  12.9 us
    unnamed x24, local copies, waits for them, and re-layouts  9.8 us
    all_gather x1, waiting for transfers between devices, per_device(): turns_a = lax.all_gather(own, 'rot', axis=0)  7.44 us
    gather x1, local copies, waits for them, and re-layouts, per_device(): tables = jnp.transpose(trans_table[dist_index], (1, 2, 0, 3))  5.39 us
    all_to_all x1, starting transfers between devices, per_device(): spread = lax.all_to_all(pieces, 'rec', 0, 0, axis_index_groups=same_core)  5.29 us
    ppermute x3, starting transfers between devices, per_device(): lax.ppermute(mine, 'rec', [(i, i ^ 2 * k) for i in range(nrec)])  3.55 us
  transfers between devices with their start and end apart: 7, of which 3 were waited for; matrix products, arithmetic and copies ran while one was open for 8% of the time, Pallas kernels for 16%

profile of v4, /device:TPU:0, one launch (start us, length us, event | category | flops | bytes accessed | tf_op | source)
XLA Modules:
  0.0 122.4 jit_solution(10511582977236003371)
XLA Ops:
  6.5 0.0 copy-start
  6.5 0.0 copy-start.6
  6.5 0.0 all-gather.4.cloned.1.call-start
  6.5 1.1 copy-done
  7.6 0.9 dynamic-slice_bitcast_fusion
  8.5 0.0 all-gather.4.cloned.1.call-update
  8.5 1.3 %copy.13 = bf16[8,2,2,15,900]{4,0,3,1,2:T(8,128)(2,1)S(1)} copy(bf16[8,2,2,15,900]{4,0,3,2,1:T(8,128)(2,1)} %bitcast.23) | data formatting | bytes 1728000 | tf_op jit(solution)/shard_map/reshape | solution.py:251
  9.8 0.0 copy-done.6
  9.8 2.3 %ligand_slots.1 = bf16[16,120,256]{2,1,0:T(8,128)(2,1)} custom-call(s32[1,1024]{1,0:T(1,128)S(1)} %copy-done.6, bf16[480,900]{1,0:T(8,128)(2,1)S(1)} %bitcast.22), custom_call_target="tpu_custom_call" | custom-call | tf_op jit(solution)/shard_map/ligand_slots/pallas_call | solution.py:253
  12.1 0.0 copy-start.9
  12.1 5.3 %all-to-all-start = ((bf16[4,480,256]{2,1,0:T(8,128)(2,1)}), bf16[4,480,256]{2,1,0:T(8,128)(2,1)S(1)}, u32[]{:S(2)}, u32[]{:S(2)}) async-start(bf16[4,480,256]{2,1,0:T(8,128)(2,1)} %bitcast.6), calls=%async_computation | async-start | bytes 1966080 | tf_op jit(solution)/shard_map/all_to_all | solution.py:260
  17.4 12.9 %all-to-all-done = bf16[4,480,256]{2,1,0:T(8,128)(2,1)S(1)} async-done(((bf16[4,480,256]{2,1,0:T(8,128)(2,1)}), bf16[4,480,256]{2,1,0:T(8,128)(2,1)S(1)}, u32[]{:S(2)}, u32[]{:S(2)}) %all-to-all-start) | async-done | bytes 983072 | tf_op jit(solution)/shard_map/all_to_all | solution.py:260
  30.4 1.5 %collective-permute-start = (bf16[480,256]{1,0:T(8,128)(2,1)S(1)}, bf16[480,256]{1,0:T(8,128)(2,1)S(1)}, u32[]{:S(2)}, u32[]{:S(2)}) collective-permute-start(bf16[480,256]{1,0:T(8,128)(2,1)S(1)} %dynamic-slice_bitcast_fusion.1), channel_id=1, source_target_pairs={{0,8},{4,12},{8,0},{12,4},{16,24},{20,28},{24,16},{28,20},{1,9},{5... | collective-permute-start | bytes 737288 | tf_op jit(solution)/shard_map/ppermute | solution.py:264
  31.8 0.6 collective-permute-start.1
  32.4 1.5 %collective-permute-start.2 = (bf16[480,256]{1,0:T(8,128)(2,1)S(1)}, bf16[480,256]{1,0:T(8,128)(2,1)S(1)}, u32[]{:S(2)}, u32[]{:S(2)}) collective-permute-start(bf16[480,256]{1,0:T(8,128)(2,1)S(1)} %dynamic-slice_bitcast_fusion.1), channel_id=1, source_target_pairs={{0,24},{4,28},{8,16},{12,20},{16,8},{20,12},{24,0},{28,4},{1,25},{... | collective-permute-start | bytes 737288 | tf_op jit(solution)/shard_map/ppermute | solution.py:264
  33.9 7.4 %all-gather.4.cloned.1.call-done.w_ref = bf16[4,4,35990]{2,1,0:T(4,128)(2,1)} async-done(((bf16[1,4,35990]{2,1,0:T(4,128)(2,1)}), bf16[4,4,35990]{2,1,0:T(4,128)(2,1)}) %all-gather.4.cloned.1.call-update) | async-done | bytes 1151696 | tf_op jit(solution)/shard_map/all_gather | solution.py:247
  41.4 0.0 collective-permute-start.4
  41.4 0.0 collective-permute-done
  41.4 2.1 %collective-permute-done.1 = bf16[480,256]{1,0:T(8,128)(2,1)S(1)} collective-permute-done((bf16[480,256]{1,0:T(8,128)(2,1)S(1)}, bf16[480,256]{1,0:T(8,128)(2,1)S(1)}, u32[]{:S(2)}, u32[]{:S(2)}) %collective-permute-start.1) | collective-permute-done | bytes 245792 | tf_op jit(solution)/shard_map/ppermute | solution.py:264
  43.4 0.0 collective-permute-done.2
  43.4 0.1 pad_maximum_fusion
  43.5 0.1 collective-permute-start.3
  43.6 0.0 copy-done.9
  43.6 1.5 %copy.12 = bf16[8,60,900]{2,1,0:T(8,128)(2,1)} copy(bf16[8,60,900]{2,0,1:T(8,128)(2,1)S(1)} %copy-done.9) | data formatting | bytes 1728000 | tf_op args[0]
  45.1 1.6 %reshape.27 = bf16[16,30,900]{2,1,0:T(8,128)(2,1)S(1)} reshape(bf16[8,60,900]{2,1,0:T(8,128)(2,1)} %copy.12) | data formatting | bytes 1728000 | tf_op jit(solution)/shard_map/reshape | solution.py:276
  46.8 0.2 pad.4
  47.0 0.0 copy-start.10
  47.0 1.6 %receptor_slots.1.rec_ref = bf16[15,64,1024]{2,1,0:T(8,128)(2,1)S(1)} custom-call(s32[1,1024]{1,0:T(1,128)S(1)} %copy-done.6, bf16[512,900]{1,0:T(8,128)(2,1)S(1)} %bitcast.19), custom_call_target="tpu_custom_call" | custom-call | tf_op jit(solution)/shard_map/receptor_slots/pallas_call | solution.py:278
  48.6 0.0 copy-start.3
  48.6 1.3 %copy-done.3 = bf16[15,64,1024]{2,1,0:T(8,128)(2,1)} copy-done((bf16[15,64,1024]{2,1,0:T(8,128)(2,1)}, bf16[15,64,1024]{2,1,0:T(8,128)(2,1)S(1)}, u32[]{:S(2)}) %copy-start.3) | copy-done | bytes 1966104
  49.9 0.0 copy-done.10
  49.9 5.4 %gather_fusion = bf16[8,30,30,30]{3,0,2,1:T(8,128)(2,1)S(1)} fusion(bf16[16,30,30,30]{3,0,2,1:T(8,128)(2,1)} %param.11, s32[1024]{0:T(1024)S(1)} %pad_clamp_fusion), kind=kCustom, calls=%fused_computation | custom fusion | bytes 864032 | tf_op jit(solution)/shard_map/gather | solution.py:284
  55.3 0.0 copy-start.5
  55.3 1.3 %copy-done.5 = bf16[4,4,35990]{2,1,0:T(4,128)(2,1)S(1)} copy-done((bf16[4,4,35990]{2,1,0:T(4,128)(2,1)S(1)}, bf16[4,4,35990]{2,1,0:T(4,128)(2,1)}, u32[]{:S(2)}) %copy-start.5) | copy-done | bytes 1151704
  56.6 7.3 %unpack.2.wig_a_ref = bf16[15,16,64,128]{3,2,1,0:T(8,128)(2,1)S(1)} custom-call(bf16[4,4,35990]{2,1,0:T(4,128)(2,1)S(1)} %copy-done.5), custom_call_target="tpu_custom_call" | custom-call | tf_op jit(solution)/shard_map/unpack/pallas_call | solution.py:128
  63.9 0.0 copy-start.1
  63.9 1.8 %copy-done.1 = bf16[15,16,64,128]{3,2,1,0:T(8,128)(2,1)} copy-done((bf16[15,16,64,128]{3,2,1,0:T(8,128)(2,1)}, bf16[15,16,64,128]{3,2,1,0:T(8,128)(2,1)S(1)}, u32[]{:S(2)}) %copy-start.1) | copy-done | bytes 3932184
  65.8 0.0 copy-start.4
  65.8 0.0 copy-start.7
  65.8 0.0 copy-start.8
  65.8 0.0 collective-permute-done.4.w_ref
  65.8 8.8 %unpack.3.wig_b_ref = bf16[15,16,64,128]{3,2,1,0:T(8,128)(2,1)S(1)} custom-call(bf16[4,4,35990]{2,1,0:T(4,128)(2,1)} %collective-permute-done.4.w_ref), custom_call_target="tpu_custom_call" | custom-call | tf_op jit(solution)/shard_map/unpack/pallas_call | solution.py:128
  74.6 0.0 copy-start.2
  74.6 1.9 %copy-done.2 = bf16[15,16,64,128]{3,2,1,0:T(8,128)(2,1)} copy-done((bf16[15,16,64,128]{3,2,1,0:T(8,128)(2,1)}, bf16[15,16,64,128]{3,2,1,0:T(8,128)(2,1)S(1)}, u32[]{:S(2)}) %copy-start.2) | copy-done | bytes 3932184
  76.5 0.0 collective-permute-done.3.lig_b_ref
  76.5 0.0 copy-done.4
  76.5 0.0 copy-done.7
  76.5 0.0 copy-done.8
  76.5 38.1 %scores.1 = f32[16,64]{1,0:T(8,128)S(1)} custom-call(s32[15]{0:T(128)S(1)} %fusion.2.where_ref, s32[15]{0:T(128)S(1)} %copy-done.7, s32[15]{0:T(128)S(1)} %copy-done.8, bf16[30,240,30]{2,1,0:T(8,128)(2,1)S(1)} %bitcast.17, bf16[30,240,30]{2,1,0:T(8,128)(2,1)S(1)} %bitcast.18, bf16[15,64,1024]{2,1,0:T(8,128)(2,1)S(1)} %copy-done.4, ...), custom_call_target="tpu_custom_call" | custom-call | tf_op jit(solution)/shard_map/scores/pallas_call | solution.py:289
  114.6 0.1 reshape.33
  114.7 0.1 reduce_sum.9
  114.8 0.7 copy.15
  (5 shorter events, 0.0 us)
Async XLA Ops:
  6.5 1.1 copy-start
  6.5 3.3 %copy-start.6 = (s32[1,1024]{1,0:T(1,128)S(1)}, s32[1,1024]{1,0:T(1,128)}, u32[]{:S(2)}) copy-start(s32[1,1024]{1,0:T(1,128)} %constant.86.source_ref) | copy-start | bytes 12292
  6.5 34.8 %all-gather.4.cloned.1.call-start = ((), (), s32[]{:S(2)}) async-start(), calls=%async_computation.1 | async-start | bytes 1443840 | tf_op jit(solution)/shard_map/all_gather | solution.py:247
  12.1 31.5 %copy-start.9 = (bf16[8,60,900]{2,0,1:T(8,128)(2,1)S(1)}, bf16[8,60,900]{2,0,1:T(8,128)(2,1)}, u32[]{:S(2)}) copy-start(bf16[8,60,900]{2,0,1:T(8,128)(2,1)} %param.8) | copy-start | bytes 2592004
  12.1 18.2 %all-to-all-start = ((bf16[4,480,256]{2,1,0:T(8,128)(2,1)}), bf16[4,480,256]{2,1,0:T(8,128)(2,1)S(1)}, u32[]{:S(2)}, u32[]{:S(2)}) async-start(bf16[4,480,256]{2,1,0:T(8,128)(2,1)} %bitcast.6), calls=%async_computation | async-start | bytes 1966080 | tf_op jit(solution)/shard_map/all_to_all | solution.py:260
  30.4 11.0 %collective-permute-start = (bf16[480,256]{1,0:T(8,128)(2,1)S(1)}, bf16[480,256]{1,0:T(8,128)(2,1)S(1)}, u32[]{:S(2)}, u32[]{:S(2)}) collective-permute-start(bf16[480,256]{1,0:T(8,128)(2,1)S(1)} %dynamic-slice_bitcast_fusion.1), channel_id=1, source_target_pairs={{0,8},{4,12},{8,0},{12,4},{16,24},{20,28},{24,16},{28,20},{1,9},{5... | collective-permute-start | bytes 737288 | tf_op jit(solution)/shard_map/ppermute | solution.py:264
  31.8 11.6 %collective-permute-start.1 = (bf16[480,256]{1,0:T(8,128)(2,1)S(1)}, bf16[480,256]{1,0:T(8,128)(2,1)S(1)}, u32[]{:S(2)}, u32[]{:S(2)}) collective-permute-start(bf16[480,256]{1,0:T(8,128)(2,1)S(1)} %dynamic-slice_bitcast_fusion.1), channel_id=1, source_target_pairs={{0,16},{4,20},{8,24},{12,28},{16,0},{20,4},{24,8},{28,12},{1,17},{... | collective-permute-start | bytes 737288 | tf_op jit(solution)/shard_map/ppermute | solution.py:264
  32.4 11.0 %collective-permute-start.2 = (bf16[480,256]{1,0:T(8,128)(2,1)S(1)}, bf16[480,256]{1,0:T(8,128)(2,1)S(1)}, u32[]{:S(2)}, u32[]{:S(2)}) collective-permute-start(bf16[480,256]{1,0:T(8,128)(2,1)S(1)} %dynamic-slice_bitcast_fusion.1), channel_id=1, source_target_pairs={{0,24},{4,28},{8,16},{12,20},{16,8},{20,12},{24,0},{28,4},{1,25},{... | collective-permute-start | bytes 737288 | tf_op jit(solution)/shard_map/ppermute | solution.py:264
  41.4 24.4 %collective-permute-start.4 = (bf16[4,4,35990]{2,1,0:T(4,128)(2,1)}, bf16[4,4,35990]{2,1,0:T(4,128)(2,1)}, u32[]{:S(2)}, u32[]{:S(2)}) collective-permute-start(bf16[4,4,35990]{2,1,0:T(4,128)(2,1)} %all-gather.4.cloned.1.call-done.w_ref), channel_id=1, source_target_pairs={{0,4},{4,0},{8,12},{12,8},{16,20},{20,16},{24,28},{28,24},{1,5},{5... | collective-permute-start | bytes 3455048 | tf_op jit(solution)/shard_map/ppermute | solution.py:248
  43.5 33.0 %collective-permute-start.3 = (bf16[16,120,256]{2,1,0:T(8,128)(2,1)S(1)}, bf16[16,120,256]{2,1,0:T(8,128)(2,1)}, u32[]{:S(2)}, u32[]{:S(2)}) collective-permute-start(bf16[16,120,256]{2,1,0:T(8,128)(2,1)S(1)} %bitcast.20), channel_id=1, source_target_pairs={{0,4},{4,0},{8,12},{12,8},{16,20},{20,16},{24,28},{28,24},{1,5},{5... | collective-permute-start | bytes 2949128 | tf_op jit(solution)/shard_map/ppermute | solution.py:266
  47.0 3.0 %copy-start.10 = (s32[8]{0:T(128)S(1)}, s32[8]{0:T(128)}, u32[]{:S(2)}) copy-start(s32[8]{0:T(128)} %param.12) | copy-start | bytes 100
  48.6 1.3 %copy-start.3 = (bf16[15,64,1024]{2,1,0:T(8,128)(2,1)}, bf16[15,64,1024]{2,1,0:T(8,128)(2,1)S(1)}, u32[]{:S(2)}) copy-start(bf16[15,64,1024]{2,1,0:T(8,128)(2,1)S(1)} %receptor_slots.1.rec_ref) | copy-start | bytes 5898244
  55.3 1.3 %copy-start.5 = (bf16[4,4,35990]{2,1,0:T(4,128)(2,1)S(1)}, bf16[4,4,35990]{2,1,0:T(4,128)(2,1)}, u32[]{:S(2)}) copy-start(bf16[4,4,35990]{2,1,0:T(4,128)(2,1)} %all-gather.4.cloned.1.call-done.w_ref) | copy-start | bytes 3455044
  63.9 1.9 %copy-start.1 = (bf16[15,16,64,128]{3,2,1,0:T(8,128)(2,1)}, bf16[15,16,64,128]{3,2,1,0:T(8,128)(2,1)S(1)}, u32[]{:S(2)}) copy-start(bf16[15,16,64,128]{3,2,1,0:T(8,128)(2,1)S(1)} %unpack.2.wig_a_ref) | copy-start | bytes 11796484
  65.8 10.7 %copy-start.4 = (bf16[15,64,1024]{2,1,0:T(8,128)(2,1)S(1)}, bf16[15,64,1024]{2,1,0:T(8,128)(2,1)}, u32[]{:S(2)}) copy-start(bf16[15,64,1024]{2,1,0:T(8,128)(2,1)} %copy-done.3) | copy-start | bytes 5898244
  65.8 10.7 %copy-start.7 = (s32[15]{0:T(128)S(1)}, s32[15]{0:T(128)}, u32[]{:S(2)}) copy-start(s32[15]{0:T(128)} %constant.82.clone.one_ref) | copy-start | bytes 184
  65.8 10.7 %copy-start.8 = (s32[15]{0:T(128)S(1)}, s32[15]{0:T(128)}, u32[]{:S(2)}) copy-start(s32[15]{0:T(128)} %constant.83.clone.two_ref) | copy-start | bytes 184
  74.6 1.9 %copy-start.2 = (bf16[15,16,64,128]{3,2,1,0:T(8,128)(2,1)}, bf16[15,16,64,128]{3,2,1,0:T(8,128)(2,1)S(1)}, u32[]{:S(2)}) copy-start(bf16[15,16,64,128]{3,2,1,0:T(8,128)(2,1)S(1)} %unpack.3.wig_b_ref) | copy-start | bytes 11796484
Sparse Core Ops, SparseCore 0:
  8.9 32.3 all-gather.3

commit v5 on v4

--- a/solution.py
+++ b/solution.py
@@ -258,19 +258,6 @@
     )(source, lig)
     pieces = lig.reshape(nrec // 2, -1, 256)
     spread = lax.all_to_all(pieces, "rec", 0, 0, axis_index_groups=same_core)
-    mine = lax.dynamic_index_in_dim(spread, lax.axis_index("rot"), 0, keepdims=False)
-    found = [mine]
-    for k in range(1, nrec // 2):
-        found.append(lax.ppermute(mine, "rec", [(i, i ^ (2 * k)) for i in range(nrec)]))
-    lig_a = jnp.concatenate(found, axis=0).reshape(padded, half * part, 256)
-    lig_b = lax.ppermute(lig_a, "rec", swap)
-    each = padded // (nrec // 2)
-    order = jnp.arange(count, dtype=jnp.int32)
-    chip = (lax.axis_index("rec") // 2).astype(jnp.int32)
-    where = (chip ^ (order // each)) * each + order % each
-
-    wig_a = unpack_wigner(turns_a, groups)
-    wig_b = unpack_wigner(turns_b, groups)
 
     deep = (radial + 15) // 16 * 16
     rec = receptors.reshape(recs * props, radial, angular)
@@ -283,6 +270,21 @@
     )(source, rec)
     tables = jnp.transpose(trans_table[dist_index], (1, 2, 0, 3))
     tables = tables.reshape(degrees, radial * dists, radial)
+    spread, rec, tables = lax.optimization_barrier((spread, rec, tables))
+    mine = lax.dynamic_index_in_dim(spread, lax.axis_index("rot"), 0, keepdims=False)
+    found = [mine]
+    for k in range(1, nrec // 2):
+        found.append(lax.ppermute(mine, "rec", [(i, i ^ (2 * k)) for i in range(nrec)]))
+    lig_a = jnp.concatenate(found, axis=0).reshape(padded, half * part, 256)
+    lig_b = lax.ppermute(lig_a, "rec", swap)
+    each = padded // (nrec // 2)
+    order = jnp.arange(count, dtype=jnp.int32)
+    chip = (lax.axis_index("rec") // 2).astype(jnp.int32)
+    where = (chip ^ (order // each)) * each + order % each
+
+    wig_a = unpack_wigner(turns_a, groups)
+    wig_b = unpack_wigner(turns_b, groups)
+
     one = jnp.array([members[0] for members in groups], jnp.int32)
     two = jnp.array([members[-1] for members in groups], jnp.int32)
 

time: 123 us -> 115 us (0.935)
  waiting for transfers between devices: 22.5 us -> 13.9 us
  other arithmetic: 0.18 us -> 1.49 us
    all_to_all x1, waiting for transfers between devices: 12.9 us -> 3.84 us  [per_device(): spread = lax.all_to_all(pieces, 'rec', 0, 0, axis_index_groups=same_core)]
    ppermute x3, waiting for transfers between devices: 2.08 us -> 4.05 us  [per_device(): lax.ppermute(mine, 'rec', [(i, i ^ 2 * k) for i in range(nrec)])]
    all_gather x1, waiting for transfers between devices: 7.44 us -> 6 us  [per_device(): turns_a = lax.all_gather(own, 'rot', axis=0)]
    concatenate x1, other arithmetic: 0.06 us -> 1.37 us  [per_device(): lig_a = jnp.concatenate(found, axis=0).reshape(padded, half * part, 256)]
    unnamed x24 -> x30, local copies, waits for them, and re-layouts: 9.8 us -> 9.5 us
  transfers between devices with their start and end apart: 7 -> 7, of which waited for: 3 -> 3; matrix products, arithmetic and copies ran while one was open for 8% -> 9% of each run, Pallas kernels for 16% -> 17%
where the time goes in v5:
time: 115 us
  Pallas kernels  58.2 us (51%)
  local copies, waits for them, and re-layouts  18.7 us (16%)
  waiting for transfers between devices  13.9 us (12%)
  between operations  13.6 us (12%)
  starting transfers between devices  8.79 us (8%)
  other arithmetic  1.49 us (1%)
    pallas_call x1, Pallas kernels, per_device(): pl.pallas_call(score_kernel, grid_spec=pltpu.PrefetchScalarGridSpec(num_s...  38.1 us
    pallas_call x2, Pallas kernels, unpack_wigner(): pl.pallas_call(functools.partial(unpack_kernel, groups), grid=(parts // b...  16.1 us
    unnamed x30, local copies, waits for them, and re-layouts  9.5 us
    all_gather x1, waiting for transfers between devices, per_device(): turns_a = lax.all_gather(own, 'rot', axis=0)  6 us
    gather x1, local copies, waits for them, and re-layouts, per_device(): tables = jnp.transpose(trans_table[dist_index], (1, 2, 0, 3))  5.42 us
    all_to_all x1, starting transfers between devices, per_device(): spread = lax.all_to_all(pieces, 'rec', 0, 0, axis_index_groups=same_core)  5.16 us
    ppermute x3, waiting for transfers between devices, per_device(): lax.ppermute(mine, 'rec', [(i, i ^ 2 * k) for i in range(nrec)])  4.05 us
    all_to_all x1, waiting for transfers between devices, per_device(): spread = lax.all_to_all(pieces, 'rec', 0, 0, axis_index_groups=same_core)  3.84 us
  transfers between devices with their start and end apart: 7, of which 3 were waited for; matrix products, arithmetic and copies ran while one was open for 9% of the time, Pallas kernels for 17%

profile of v5, /device:TPU:0, one launch (start us, length us, event | category | flops | bytes accessed | tf_op | source)
XLA Modules:
  0.0 114.6 jit_solution(12540557636319598413)
XLA Ops:
  6.5 0.0 copy-start
  6.5 0.0 copy-start.6
  6.5 0.0 all-gather.4.cloned.1.call-start
  6.5 1.1 copy-done
  7.6 0.9 dynamic-slice_bitcast_fusion
  8.5 0.0 all-gather.4.cloned.1.call-update
  8.5 1.3 %copy.12 = bf16[8,2,2,15,900]{4,0,3,1,2:T(8,128)(2,1)S(1)} copy(bf16[8,2,2,15,900]{4,0,3,2,1:T(8,128)(2,1)} %bitcast.23) | data formatting | bytes 1728000 | tf_op jit(solution)/shard_map/reshape | solution.py:251
  9.8 0.0 copy-done.6
  9.8 0.0 copy-start.10
  9.8 2.3 %ligand_slots.1 = bf16[16,120,256]{2,1,0:T(8,128)(2,1)} custom-call(s32[1,1024]{1,0:T(1,128)S(1)} %copy-done.6, bf16[480,900]{1,0:T(8,128)(2,1)S(1)} %bitcast.22), custom_call_target="tpu_custom_call" | custom-call | tf_op jit(solution)/shard_map/ligand_slots/pallas_call | solution.py:253
  12.1 5.2 %all-to-all-start = ((bf16[4,480,256]{2,1,0:T(8,128)(2,1)}), bf16[4,480,256]{2,1,0:T(8,128)(2,1)}, u32[]{:S(2)}, u32[]{:S(2)}) async-start(bf16[4,480,256]{2,1,0:T(8,128)(2,1)} %bitcast.3), calls=%async_computation | async-start | bytes 1966080 | tf_op jit(solution)/shard_map/all_to_all | solution.py:260
  17.3 0.0 copy-done.10
  17.3 0.5 copy.13
  17.8 0.6 reshape.29
  18.4 0.2 pad.4
  18.6 0.0 copy-start.13
  18.6 1.6 %receptor_slots.1.rec_ref = bf16[15,64,1024]{2,1,0:T(8,128)(2,1)S(1)} custom-call(s32[1,1024]{1,0:T(1,128)S(1)} %copy-done.6, bf16[512,900]{1,0:T(8,128)(2,1)S(1)} %bitcast.19), custom_call_target="tpu_custom_call" | custom-call | tf_op jit(solution)/shard_map/receptor_slots/pallas_call | solution.py:265
  20.2 0.0 copy-start.3
  20.2 1.3 %copy-done.3 = bf16[15,64,1024]{2,1,0:T(8,128)(2,1)} copy-done((bf16[15,64,1024]{2,1,0:T(8,128)(2,1)}, bf16[15,64,1024]{2,1,0:T(8,128)(2,1)S(1)}, u32[]{:S(2)}) %copy-start.3) | copy-done | bytes 1966104
  21.5 0.0 copy-done.13
  21.6 5.4 %gather_fusion = bf16[8,30,30,30]{3,0,2,1:T(8,128)(2,1)S(1)} fusion(bf16[16,30,30,30]{3,0,2,1:T(8,128)(2,1)} %param.11, s32[1024]{0:T(1024)S(1)} %pad_clamp_fusion), kind=kCustom, calls=%fused_computation | custom fusion | bytes 864032 | tf_op jit(solution)/shard_map/gather | solution.py:271
  27.0 3.8 %all-to-all-done = bf16[4,480,256]{2,1,0:T(8,128)(2,1)} async-done(((bf16[4,480,256]{2,1,0:T(8,128)(2,1)}), bf16[4,480,256]{2,1,0:T(8,128)(2,1)}, u32[]{:S(2)}, u32[]{:S(2)}) %all-to-all-start) | async-done | bytes 983072 | tf_op jit(solution)/shard_map/all_to_all | solution.py:260
  30.8 1.0 dynamic-slice_bitcast_fusion.1
  31.8 0.0 copy-start.9
  31.8 1.5 %collective-permute-start = (bf16[480,256]{1,0:T(8,128)(2,1)S(1)}, bf16[480,256]{1,0:T(8,128)(2,1)S(1)}, u32[]{:S(2)}, u32[]{:S(2)}) collective-permute-start(bf16[480,256]{1,0:T(8,128)(2,1)S(1)} %dynamic-slice_bitcast_fusion.1), channel_id=1, source_target_pairs={{0,8},{4,12},{8,0},{12,4},{16,24},{20,28},{24,16},{28,20},{1,9},{5... | collective-permute-start | bytes 737288 | tf_op jit(solution)/shard_map/ppermute | solution.py:277
  33.3 0.5 collective-permute-start.1
  33.9 1.5 %collective-permute-start.2 = (bf16[480,256]{1,0:T(8,128)(2,1)S(1)}, bf16[480,256]{1,0:T(8,128)(2,1)}, u32[]{:S(2)}, u32[]{:S(2)}) collective-permute-start(bf16[480,256]{1,0:T(8,128)(2,1)S(1)} %dynamic-slice_bitcast_fusion.1), channel_id=1, source_target_pairs={{0,24},{4,28},{8,16},{12,20},{16,8},{20,12},{24,0},{28,4},{1,25},{... | collective-permute-start | bytes 737288 | tf_op jit(solution)/shard_map/ppermute | solution.py:277
  35.4 6.0 %all-gather.4.cloned.1.call-done.w_ref = bf16[4,4,35990]{2,1,0:T(4,128)(2,1)} async-done(((bf16[1,4,35990]{2,1,0:T(4,128)(2,1)}), bf16[4,4,35990]{2,1,0:T(4,128)(2,1)}) %all-gather.4.cloned.1.call-update) | async-done | bytes 1151696 | tf_op jit(solution)/shard_map/all_gather | solution.py:247
  41.4 0.0 collective-permute-start.4
  41.4 0.0 collective-permute-done
  41.4 0.0 copy-start.11
  41.4 4.0 %collective-permute-done.1 = bf16[480,256]{1,0:T(8,128)(2,1)S(1)} collective-permute-done((bf16[480,256]{1,0:T(8,128)(2,1)S(1)}, bf16[480,256]{1,0:T(8,128)(2,1)S(1)}, u32[]{:S(2)}, u32[]{:S(2)}) %collective-permute-start.1) | collective-permute-done | bytes 245792 | tf_op jit(solution)/shard_map/ppermute | solution.py:277
  45.4 0.0 copy-done.9
  45.4 0.0 copy-done.11
  45.4 0.0 copy-start.12
  45.4 0.7 copy-done.12
  46.1 0.0 collective-permute-done.2
  46.1 1.4 %pad_maximum_fusion = bf16[1920,256]{1,0:T(8,128)(2,1)S(1)} fusion(bf16[480,256]{1,0:T(8,128)(2,1)} %collective-permute-done.2, bf16[480,256]{1,0:T(8,128)(2,1)} %copy-done.12, bf16[480,256]{1,0:T(8,128)(2,1)} %copy-done.11, bf16[480,256]{1,0:T(8,128)(2,1)} %copy-done.9), kind=kLoop, calls=%fused_computation.1 | loop fusion | flops 3932160 | bytes 1966080 | tf_op jit(solution)/shard_map/concatenate | solution.py:278
  47.5 0.1 collective-permute-start.3
  47.6 0.0 copy-start.5
  47.6 1.3 %copy-done.5 = bf16[4,4,35990]{2,1,0:T(4,128)(2,1)S(1)} copy-done((bf16[4,4,35990]{2,1,0:T(4,128)(2,1)S(1)}, bf16[4,4,35990]{2,1,0:T(4,128)(2,1)}, u32[]{:S(2)}) %copy-start.5) | copy-done | bytes 1151704
  48.9 7.3 %unpack.2.wig_a_ref = bf16[15,16,64,128]{3,2,1,0:T(8,128)(2,1)S(1)} custom-call(bf16[4,4,35990]{2,1,0:T(4,128)(2,1)S(1)} %copy-done.5), custom_call_target="tpu_custom_call" | custom-call | tf_op jit(solution)/shard_map/unpack/pallas_call | solution.py:128
  56.2 0.0 copy-start.1
  56.2 1.8 %copy-done.1 = bf16[15,16,64,128]{3,2,1,0:T(8,128)(2,1)} copy-done((bf16[15,16,64,128]{3,2,1,0:T(8,128)(2,1)}, bf16[15,16,64,128]{3,2,1,0:T(8,128)(2,1)S(1)}, u32[]{:S(2)}) %copy-start.1) | copy-done | bytes 3932184
  58.1 0.0 copy-start.4
  58.1 0.0 copy-start.7
  58.1 0.0 copy-start.8
  58.1 0.0 collective-permute-done.4.w_ref
  58.1 8.8 %unpack.3.wig_b_ref = bf16[15,16,64,128]{3,2,1,0:T(8,128)(2,1)S(1)} custom-call(bf16[4,4,35990]{2,1,0:T(4,128)(2,1)} %collective-permute-done.4.w_ref), custom_call_target="tpu_custom_call" | custom-call | tf_op jit(solution)/shard_map/unpack/pallas_call | solution.py:128
  66.9 0.0 copy-start.2
  66.9 1.9 %copy-done.2 = bf16[15,16,64,128]{3,2,1,0:T(8,128)(2,1)} copy-done((bf16[15,16,64,128]{3,2,1,0:T(8,128)(2,1)}, bf16[15,16,64,128]{3,2,1,0:T(8,128)(2,1)S(1)}, u32[]{:S(2)}) %copy-start.2) | copy-done | bytes 3932184
  68.8 0.0 collective-permute-done.3.lig_b_ref
  68.8 0.0 copy-done.4
  68.8 0.0 copy-done.7
  68.8 0.0 copy-done.8
  68.8 38.1 %scores.1 = f32[16,64]{1,0:T(8,128)S(1)} custom-call(s32[15]{0:T(128)S(1)} %fusion.2.where_ref, s32[15]{0:T(128)S(1)} %copy-done.7, s32[15]{0:T(128)S(1)} %copy-done.8, bf16[30,240,30]{2,1,0:T(8,128)(2,1)S(1)} %bitcast.17, bf16[30,240,30]{2,1,0:T(8,128)(2,1)S(1)} %bitcast.18, bf16[15,64,1024]{2,1,0:T(8,128)(2,1)S(1)} %copy-done.4, ...), custom_call_target="tpu_custom_call" | custom-call | tf_op jit(solution)/shard_map/scores/pallas_call | solution.py:291
  106.9 0.1 reshape.33
  107.0 0.1 reduce_sum.9
  107.1 0.7 copy.15
  (4 shorter events, 0.0 us)
Async XLA Ops:
  6.5 1.1 copy-start
  6.5 3.2 %copy-start.6 = (s32[1,1024]{1,0:T(1,128)S(1)}, s32[1,1024]{1,0:T(1,128)}, u32[]{:S(2)}) copy-start(s32[1,1024]{1,0:T(1,128)} %constant.86.source_ref) | copy-start | bytes 12292
  6.5 34.8 %all-gather.4.cloned.1.call-start = ((), (), s32[]{:S(2)}) async-start(), calls=%async_computation.1 | async-start | bytes 1443840 | tf_op jit(solution)/shard_map/all_gather | solution.py:247
  9.8 7.5 %copy-start.10 = (bf16[8,60,900]{2,0,1:T(8,128)(2,1)S(1)}, bf16[8,60,900]{2,0,1:T(8,128)(2,1)}, u32[]{:S(2)}) copy-start(bf16[8,60,900]{2,0,1:T(8,128)(2,1)} %param.8) | copy-start | bytes 2592004
  12.1 18.7 %all-to-all-start = ((bf16[4,480,256]{2,1,0:T(8,128)(2,1)}), bf16[4,480,256]{2,1,0:T(8,128)(2,1)}, u32[]{:S(2)}, u32[]{:S(2)}) async-start(bf16[4,480,256]{2,1,0:T(8,128)(2,1)} %bitcast.3), calls=%async_computation | async-start | bytes 1966080 | tf_op jit(solution)/shard_map/all_to_all | solution.py:260
  18.6 3.0 %copy-start.13 = (s32[8]{0:T(128)S(1)}, s32[8]{0:T(128)}, u32[]{:S(2)}) copy-start(s32[8]{0:T(128)} %param.12) | copy-start | bytes 100
  20.2 1.3 %copy-start.3 = (bf16[15,64,1024]{2,1,0:T(8,128)(2,1)}, bf16[15,64,1024]{2,1,0:T(8,128)(2,1)S(1)}, u32[]{:S(2)}) copy-start(bf16[15,64,1024]{2,1,0:T(8,128)(2,1)S(1)} %receptor_slots.1.rec_ref) | copy-start | bytes 5898244
  31.8 13.6 %copy-start.9 = (bf16[480,256]{1,0:T(8,128)(2,1)}, bf16[480,256]{1,0:T(8,128)(2,1)S(1)}, u32[]{:S(2)}) copy-start(bf16[480,256]{1,0:T(8,128)(2,1)S(1)} %dynamic-slice_bitcast_fusion.1) | copy-start | bytes 737284
  31.8 9.6 %collective-permute-start = (bf16[480,256]{1,0:T(8,128)(2,1)S(1)}, bf16[480,256]{1,0:T(8,128)(2,1)S(1)}, u32[]{:S(2)}, u32[]{:S(2)}) collective-permute-start(bf16[480,256]{1,0:T(8,128)(2,1)S(1)} %dynamic-slice_bitcast_fusion.1), channel_id=1, source_target_pairs={{0,8},{4,12},{8,0},{12,4},{16,24},{20,28},{24,16},{28,20},{1,9},{5... | collective-permute-start | bytes 737288 | tf_op jit(solution)/shard_map/ppermute | solution.py:277
  33.3 12.1 %collective-permute-start.1 = (bf16[480,256]{1,0:T(8,128)(2,1)S(1)}, bf16[480,256]{1,0:T(8,128)(2,1)S(1)}, u32[]{:S(2)}, u32[]{:S(2)}) collective-permute-start(bf16[480,256]{1,0:T(8,128)(2,1)S(1)} %dynamic-slice_bitcast_fusion.1), channel_id=1, source_target_pairs={{0,16},{4,20},{8,24},{12,28},{16,0},{20,4},{24,8},{28,12},{1,17},{... | collective-permute-start | bytes 737288 | tf_op jit(solution)/shard_map/ppermute | solution.py:277
  33.9 12.2 %collective-permute-start.2 = (bf16[480,256]{1,0:T(8,128)(2,1)S(1)}, bf16[480,256]{1,0:T(8,128)(2,1)}, u32[]{:S(2)}, u32[]{:S(2)}) collective-permute-start(bf16[480,256]{1,0:T(8,128)(2,1)S(1)} %dynamic-slice_bitcast_fusion.1), channel_id=1, source_target_pairs={{0,24},{4,28},{8,16},{12,20},{16,8},{20,12},{24,0},{28,4},{1,25},{... | collective-permute-start | bytes 737288 | tf_op jit(solution)/shard_map/ppermute | solution.py:277
  41.4 16.7 %collective-permute-start.4 = (bf16[4,4,35990]{2,1,0:T(4,128)(2,1)}, bf16[4,4,35990]{2,1,0:T(4,128)(2,1)}, u32[]{:S(2)}, u32[]{:S(2)}) collective-permute-start(bf16[4,4,35990]{2,1,0:T(4,128)(2,1)} %all-gather.4.cloned.1.call-done.w_ref), channel_id=1, source_target_pairs={{0,4},{4,0},{8,12},{12,8},{16,20},{20,16},{24,28},{28,24},{1,5},{5... | collective-permute-start | bytes 3455048 | tf_op jit(solution)/shard_map/ppermute | solution.py:248
  41.4 4.0 %copy-start.11 = (bf16[480,256]{1,0:T(8,128)(2,1)}, bf16[480,256]{1,0:T(8,128)(2,1)S(1)}, u32[]{:S(2)}) copy-start(bf16[480,256]{1,0:T(8,128)(2,1)S(1)} %collective-permute-done) | copy-start | bytes 737284
  45.4 0.7 copy-start.12
  47.5 21.3 %collective-permute-start.3 = (bf16[16,120,256]{2,1,0:T(8,128)(2,1)S(1)}, bf16[16,120,256]{2,1,0:T(8,128)(2,1)}, u32[]{:S(2)}, u32[]{:S(2)}) collective-permute-start(bf16[16,120,256]{2,1,0:T(8,128)(2,1)S(1)} %bitcast.20), channel_id=1, source_target_pairs={{0,4},{4,0},{8,12},{12,8},{16,20},{20,16},{24,28},{28,24},{1,5},{5... | collective-permute-start | bytes 2949128 | tf_op jit(solution)/shard_map/ppermute | solution.py:279
  47.6 1.3 %copy-start.5 = (bf16[4,4,35990]{2,1,0:T(4,128)(2,1)S(1)}, bf16[4,4,35990]{2,1,0:T(4,128)(2,1)}, u32[]{:S(2)}) copy-start(bf16[4,4,35990]{2,1,0:T(4,128)(2,1)} %all-gather.4.cloned.1.call-done.w_ref) | copy-start | bytes 3455044
  56.2 1.9 %copy-start.1 = (bf16[15,16,64,128]{3,2,1,0:T(8,128)(2,1)}, bf16[15,16,64,128]{3,2,1,0:T(8,128)(2,1)S(1)}, u32[]{:S(2)}) copy-start(bf16[15,16,64,128]{3,2,1,0:T(8,128)(2,1)S(1)} %unpack.2.wig_a_ref) | copy-start | bytes 11796484
  58.1 10.7 %copy-start.4 = (bf16[15,64,1024]{2,1,0:T(8,128)(2,1)S(1)}, bf16[15,64,1024]{2,1,0:T(8,128)(2,1)}, u32[]{:S(2)}) copy-start(bf16[15,64,1024]{2,1,0:T(8,128)(2,1)} %copy-done.3) | copy-start | bytes 5898244
  58.1 10.7 %copy-start.7 = (s32[15]{0:T(128)S(1)}, s32[15]{0:T(128)}, u32[]{:S(2)}) copy-start(s32[15]{0:T(128)} %constant.82.clone.one_ref) | copy-start | bytes 184
  58.1 10.7 %copy-start.8 = (s32[15]{0:T(128)S(1)}, s32[15]{0:T(128)}, u32[]{:S(2)}) copy-start(s32[15]{0:T(128)} %constant.83.clone.two_ref) | copy-start | bytes 184
  66.9 1.9 %copy-start.2 = (bf16[15,16,64,128]{3,2,1,0:T(8,128)(2,1)}, bf16[15,16,64,128]{3,2,1,0:T(8,128)(2,1)S(1)}, u32[]{:S(2)}) copy-start(bf16[15,16,64,128]{3,2,1,0:T(8,128)(2,1)S(1)} %unpack.3.wig_b_ref) | copy-start | bytes 11796484
Sparse Core Ops, SparseCore 0:
  8.9 32.3 all-gather.3
